TPU v7x, 256 devices: a whole 4x4x8 slice. The times are simulated.
256 devices in a mesh: leaf: 32 (over x, z), heads: 2 (over core), dp: 4 (over y).
Axes of the slice: x: 4, y: 4, z: 8, core: 2. Of those that a mesh axis runs over, the one named last changes fastest.
Arguments:
- inputs: bfloat16 [128, 256, 8192], P(('dp', 'leaf'), None, 'heads'), parts along dimension 0, may hold values from -6 to 6
- dt_raw: float32 [128, 128, 256], P(('dp', 'leaf'), 'heads'), parts along dimension 0, may hold values from -3 to 7
- b_proj: bfloat16 [128, 256, 512], P(('dp', 'leaf'), None, 'heads'), parts along dimension 0, may hold values from -6 to 6
- c_proj: bfloat16 [128, 256, 512], P(('dp', 'leaf'), None, 'heads'), parts along dimension 0, may hold values from -6 to 6
- a_log: float32 [128], P('heads'), may hold values from -1.2 to 2.3
- dt_bias: float32 [128], P('heads'), may hold values from -6.5 to -5
- skip: float32 [128], P('heads'), may hold values from 0.5 to 1.5
- grad_out: bfloat16 [128, 256, 8192], P(('dp', 'leaf'), None, 'heads'), parts along dimension 0, may hold values from -6 to 6
- parent: int32 [128], P('dp'), parts along dimension 0, may hold values from -1 to 31, as said below
- children: int32 [128, 12], P('dp'), parts along dimension 0, may hold values from -1 to 31, as said below
Outputs:
- grad_inputs: bfloat16 [128, 256, 8192], P(('dp', 'leaf'), None, 'heads'), parts along dimension 0
- grad_dt: float32 [128, 128, 256], P(('dp', 'leaf'), 'heads'), parts along dimension 0
- grad_b: float32 [128, 256, 512], P(('dp', 'leaf'), None, 'heads'), parts along dimension 0
- grad_c: float32 [128, 256, 512], P(('dp', 'leaf'), None, 'heads'), parts along dimension 0
There are 4 independent parts, one for each index of `dp`. A program takes and returns all parts, laid end to end along the dimension named above; an argument that names none is the same for every part. Nothing has to cross between parts.
Inputs may be any that keep to these rules, and one draw needn't show every extreme that they name: parent[n] is the segment whose end state starts segment n, -1 for the single root; every path from a segment up to the root holds at most 3 segments; some segment has exactly 12 children, and none has more. children[n] lists, in some order, every segment m with parent[m] = n, followed by -1 in the rest of its 12 entries.
All inputs are finite; a program needn't handle non-finite values.
Results may differ from a plain program's by a relative error of at most 0.012.
Values sent between devices are 32-bit elements; how exact they have to be, the bound alone decides.
A program may use at most 128 MiB of HBM per device.

v0:
```python
import jax
import jax.numpy as jnp
from jax import lax
from jax.sharding import PartitionSpec as P

HEAD_DIM = 64
STATE = 128
H_BLOCK = 16
TREE_DEPTH = 3


highest = lax.Precision.HIGHEST


def lowered(values):
    return values.astype(jnp.bfloat16)


def prepare(raw_block, alog_block, bias_block):
    step_rate = jax.nn.softplus(raw_block + bias_block[:, None])
    total_log = jnp.cumsum(-jnp.exp(alog_block)[:, None] * step_rate, axis=1)
    return (step_rate, total_log)


def intra_terms(x_block, raw_block, b_block, c_block, alog_block, bias_block, skip_block):
    step_rate, total_log = prepare(raw_block, alog_block, bias_block)
    length = x_block.shape[0]
    row_index = lax.broadcasted_iota(jnp.int32, (length, length), 0)
    col_index = lax.broadcasted_iota(jnp.int32, (length, length), 1)
    causal = (row_index >= col_index)[None]
    log_gap = total_log[:, :, None] - total_log[:, None, :]
    decay_mat = jnp.where(causal, jnp.exp(jnp.where(causal, log_gap, 0.0)), 0.0)
    key_dot = jnp.dot(lowered(c_block), lowered(b_block).T, preferred_element_type=jnp.float32)
    mixing = lowered(decay_mat * key_dot[None] * step_rate[:, None, :])
    result = jnp.einsum(
        "hts,shp->thp", mixing, lowered(x_block), preferred_element_type=jnp.float32
    )
    return result + skip_block[None, :, None] * x_block


def state_terms(x_block, raw_block, b_block, c_block, start_block, alog_block, bias_block):
    step_rate, total_log = prepare(raw_block, alog_block, bias_block)
    growth = jnp.exp(total_log)
    carried = growth.T[:, :, None] * jnp.einsum(
        "tn,hpn->thp", c_block, start_block, precision=highest
    )
    tail_weight = jnp.exp(total_log[:, -1:] - total_log) * step_rate
    weighted = lowered(x_block * tail_weight.T[:, :, None])
    end_state = growth[:, -1][:, None, None] * start_block + jnp.einsum(
        "shp,sn->hpn", weighted, lowered(b_block), preferred_element_type=jnp.float32
    )
    return (carried, end_state)


def summary(x_block, raw_block, b_block, c_block, dy_block, alog_block, bias_block):
    step_rate, total_log = prepare(raw_block, alog_block, bias_block)
    growth = jnp.exp(total_log)
    tail_weight = jnp.exp(total_log[:, -1:] - total_log) * step_rate
    weighted = lowered(x_block * tail_weight.T[:, :, None])
    local_end = jnp.einsum(
        "shp,sn->hpn", weighted, lowered(b_block), preferred_element_type=jnp.float32
    )
    pulled_rows = lowered(dy_block * growth.T[:, :, None])
    pulled = jnp.einsum(
        "thp,tn->hpn", pulled_rows, lowered(c_block), preferred_element_type=jnp.float32
    )
    return (local_end, growth[:, -1], pulled)


def whole_grads(
    x_block,
    raw_block,
    b_block,
    c_block,
    dy_block,
    start_block,
    grad_block,
    alog_block,
    bias_block,
    skip_block,
):

    def combined(x_in, raw_in, b_in, c_in):
        carried, end_state = state_terms(
            x_in, raw_in, b_in, c_in, start_block, alog_block, bias_block
        )
        return (
            intra_terms(x_in, raw_in, b_in, c_in, alog_block, bias_block, skip_block) + carried,
            end_state,
        )

    unused, pullback = jax.vjp(combined, x_block, raw_block, b_block, c_block)
    return pullback((dy_block, grad_block))


def forward_tree(own_end, carries, link_up):
    node_count = own_end.shape[0]
    start_state = jnp.zeros_like(own_end)
    for depth_step in range(TREE_DEPTH - 1):
        finish = carries * start_state + own_end
        start_state = jnp.dot(link_up, finish.reshape(node_count, -1), precision=highest).reshape(
            own_end.shape
        )
    return start_state


def backward_tree(own_pull, carries, link_down):
    node_count = own_pull.shape[0]
    end_grad = jnp.zeros_like(own_pull)
    for depth_step in range(TREE_DEPTH - 1):
        start_grad = own_pull + carries * end_grad
        end_grad = jnp.dot(
            link_down, start_grad.reshape(node_count, -1), precision=highest
        ).reshape(own_pull.shape)
    return end_grad


def to_slices(payload):
    return lax.all_to_all(payload, "leaf", split_axis=0, concat_axis=0, tiled=True)


def to_nodes(payload):
    return lax.all_to_all(payload, "leaf", split_axis=0, concat_axis=0, tiled=True)


def body(inputs, dt_raw, b_proj, c_proj, a_log, dt_bias, skip, grad_out, parent, children):
    length = inputs.shape[1]
    heads_here = a_log.shape[0]
    blocks = heads_here // H_BLOCK
    groups_here = b_proj.shape[2] // STATE
    per_group = blocks // groups_here
    node_count = parent.shape[0]
    state_size = HEAD_DIM * STATE
    x_blocks = inputs[0].reshape(length, blocks, H_BLOCK, HEAD_DIM).transpose(1, 0, 2, 3)
    dy_blocks = grad_out[0].reshape(length, blocks, H_BLOCK, HEAD_DIM).transpose(1, 0, 2, 3)
    raw_blocks = dt_raw[0].reshape(blocks, H_BLOCK, length)
    b_blocks = jnp.repeat(
        b_proj[0].reshape(length, groups_here, STATE).transpose(1, 0, 2), per_group, axis=0
    )
    c_blocks = jnp.repeat(
        c_proj[0].reshape(length, groups_here, STATE).transpose(1, 0, 2), per_group, axis=0
    )
    alog_blocks = a_log.reshape(blocks, H_BLOCK)
    bias_blocks = dt_bias.reshape(blocks, H_BLOCK)
    skip_blocks = skip.reshape(blocks, H_BLOCK)

    def first_block(members):
        x_block = members[0].astype(jnp.float32)
        raw_block = members[1]
        b_block = members[2].astype(jnp.float32)
        c_block = members[3].astype(jnp.float32)
        dy_block = members[4].astype(jnp.float32)
        alog_block, bias_block, skip_block = (members[5], members[6], members[7])
        local_end, carried_out, pulled = summary(
            x_block, raw_block, b_block, c_block, dy_block, alog_block, bias_block
        )
        return (local_end, carried_out, pulled)

    firsts = lax.map(
        first_block,
        (
            x_blocks,
            raw_blocks,
            b_blocks,
            c_blocks,
            dy_blocks,
            alog_blocks,
            bias_blocks,
            skip_blocks,
        ),
    )
    own_end = firsts[0].reshape(heads_here, state_size)
    carries = firsts[1].reshape(heads_here, 1)
    own_pull = firsts[2].reshape(heads_here, state_size)
    node_ids = jnp.arange(node_count, dtype=jnp.int32)
    link_up = (parent[:, None] == node_ids[None, :]).astype(jnp.float32)
    link_down = jnp.any(children[:, :, None] == node_ids[None, None, :], axis=1).astype(jnp.float32)

    def as_slices(flat):
        return flat.reshape(node_count, heads_here // node_count, -1)

    end_slices, carry_slices = to_slices((own_end, carries))
    carry_slices = as_slices(carry_slices)
    start_slices = forward_tree(as_slices(end_slices), carry_slices, link_up)
    start_state = to_nodes(start_slices.reshape(heads_here, state_size))
    pull_slices = to_slices(own_pull)
    grad_slices = backward_tree(as_slices(pull_slices), carry_slices, link_down)
    end_grad = to_nodes(grad_slices.reshape(heads_here, state_size))
    start_blocks = start_state.reshape(blocks, H_BLOCK, HEAD_DIM, STATE)
    grad_blocks = end_grad.reshape(blocks, H_BLOCK, HEAD_DIM, STATE)

    def second_block(members):
        x_block = members[0].astype(jnp.float32)
        raw_block = members[1]
        b_block = members[2].astype(jnp.float32)
        c_block = members[3].astype(jnp.float32)
        dy_block = members[4].astype(jnp.float32)
        start_block, grad_block = (members[5], members[6])
        alog_block, bias_block, skip_block = (members[7], members[8], members[9])
        return whole_grads(
            x_block,
            raw_block,
            b_block,
            c_block,
            dy_block,
            start_block,
            grad_block,
            alog_block,
            bias_block,
            skip_block,
        )

    seconds = lax.map(
        second_block,
        (
            x_blocks,
            raw_blocks,
            b_blocks,
            c_blocks,
            dy_blocks,
            start_blocks,
            grad_blocks,
            alog_blocks,
            bias_blocks,
            skip_blocks,
        ),
    )
    grad_x, grad_raw, grad_bb, grad_cb = seconds
    grad_inputs = (
        grad_x.transpose(1, 0, 2, 3).reshape(1, length, heads_here * HEAD_DIM).astype(jnp.bfloat16)
    )
    grad_dt = grad_raw.reshape(1, heads_here, length)
    grad_b = (
        grad_bb.reshape(groups_here, per_group, length, STATE)
        .sum(axis=1)
        .transpose(1, 0, 2)
        .reshape(1, length, groups_here * STATE)
    )
    grad_c = (
        grad_cb.reshape(groups_here, per_group, length, STATE)
        .sum(axis=1)
        .transpose(1, 0, 2)
        .reshape(1, length, groups_here * STATE)
    )
    return (grad_inputs, grad_dt, grad_b, grad_c)


def solution(mesh):
    placed = (
        P(("dp", "leaf"), None, "heads"),
        P(("dp", "leaf"), "heads", None),
        P(("dp", "leaf"), None, "heads"),
        P(("dp", "leaf"), None, "heads"),
        P("heads"),
        P("heads"),
        P("heads"),
        P(("dp", "leaf"), None, "heads"),
        P("dp"),
        P("dp", None),
    )
    return jax.shard_map(
        body,
        mesh=mesh,
        in_specs=placed,
        out_specs=(
            P(("dp", "leaf"), None, "heads"),
            P(("dp", "leaf"), "heads", None),
            P(("dp", "leaf"), None, "heads"),
            P(("dp", "leaf"), None, "heads"),
        ),
        check_vma=False,
    )
```

profile of v0, /device:TPU:16, one launch (start us, length us, event | category | flops | bytes accessed | tf_op | source)
XLA Modules:
  0.0 412.6 jit_solution(18434959236540484959)
XLA Ops:
  0.7 3.3 copy.194
  4.0 4.2 %copy.197 = bf16[1,256,4096]{1,2,0:T(8,128)(2,1)} copy(bf16[1,256,4096]{2,1,0:T(8,128)(2,1)} %param.15) | data formatting | bytes 4194304 | tf_op args[0]
  8.7 19.2 %while.30 = (s32[]{:T(128)}, f32[4,16,64,128]{3,2,1,0:T(8,128)}, f32[4,16]{1,0:T(4,128)S(1)}, f32[4,16,64,128]{3,2,1,0:T(8,128)}, bf16[4,256,16,64]{1,3,2,0:T(8,...) while((s32[]{:T(128)}, f32[4,16,64,128]{3,2,1,0:T(8,128)}, ...), condition=%wide.region_3.4_spmd, body=%wide.region_0.3_spmd.sunk | while | flops 136388672 | bytes 2511965 | solution.py:159
  11.1 2.1 fusion.192
  15.9 2.1 fusion.192
  20.7 2.2 fusion.192
  25.5 2.1 fusion.192
  28.5 11.3 %all-to-all-start.1 = ((f32[32,2,1]{1,2,0:T(1,128)}), f32[32,2,1]{1,2,0:T(1,128)S(1)}, u32[]{:S(2)}, u32[]{:S(2)}) async-start(f32[32,2,1]{1,2,0:T(1,128)} %bitcast.53), calls=%async_computation.1 | async-start | bytes 32768 | tf_op jit(solution)/shard_map/all_to_all | solution.py:119
  39.9 3.5 all_to_all.26
  43.3 6.2 %all-to-all-done.1 = f32[32,2,1]{1,2,0:T(1,128)S(1)} async-done(((f32[32,2,1]{1,2,0:T(1,128)}), f32[32,2,1]{1,2,0:T(1,128)S(1)}, u32[]{:S(2)}, u32[]{:S(2)}) %all-to-all-start.1) | async-done | bytes 288 | tf_op jit(solution)/shard_map/all_to_all | solution.py:119
  49.6 4.8 %all-to-all-start = ((f32[32,2,8192]{2,1,0:T(2,128)}), f32[32,2,8192]{2,1,0:T(2,128)}, u32[]{:S(2)}, u32[]{:S(2)}) async-start(f32[32,2,8192]{2,1,0:T(2,128)} %all_to_all.26), calls=%async_computation | async-start | bytes 4194304 | tf_op jit(solution)/shard_map/all_to_all | solution.py:119
  54.3 3.4 all_to_all.31
  57.8 45.7 %all-to-all-done = f32[32,2,8192]{2,1,0:T(2,128)} async-done(((f32[32,2,8192]{2,1,0:T(2,128)}), f32[32,2,8192]{2,1,0:T(2,128)}, u32[]{:S(2)}, u32[]{:S(2)}) %all-to-all-start) | async-done | bytes 2097184 | tf_op jit(solution)/shard_map/all_to_all | solution.py:119
  103.5 6.2 %all-to-all-start.3 = ((f32[32,2,8192]{2,1,0:T(2,128)}), f32[32,2,8192]{2,1,0:T(2,128)}, u32[]{:S(2)}, u32[]{:S(2)}) async-start(f32[32,2,8192]{2,1,0:T(2,128)} %all_to_all.31), calls=%async_computation.3 | async-start | bytes 4194304 | tf_op jit(solution)/shard_map/all_to_all | solution.py:119
  110.0 49.1 %all-to-all-done.3 = f32[32,2,8192]{2,1,0:T(2,128)} async-done(((f32[32,2,8192]{2,1,0:T(2,128)}), f32[32,2,8192]{2,1,0:T(2,128)}, u32[]{:S(2)}, u32[]{:S(2)}) %all-to-all-start.3) | async-done | bytes 2097184 | tf_op jit(solution)/shard_map/all_to_all | solution.py:119
  159.1 5.9 %broadcast_add_fusion = (f32[32,2,8192]{2,1,0:T(2,128)}, f32[32,2,8192]{2,1,0:T(2,128)S(1)}) fusion(f32[32,2,8192]{2,1,0:T(2,128)} %all-to-all-done.3, f32[32,2]{1,0:T(8,128)S(1)} %copy.200, f32[32,2,8192]{2,1,0:T(2,128)} %all-to-all-done), kind=kLoop, calls=%fused_computation.201 | loop fusion | flops 1048576 | bytes 8388864 | tf_op jit(solution)/shard_map/add | solution.py:100
  165.0 5.3 %fusion.127 = f32[2,4,8,8192]{3,2,1,0:T(8,128)S(1)} fusion(f32[32,2,8192]{2,1,0:T(2,128)} %all-to-all-done, f32[32,2]{0,1:T(2,128)S(1)} %bitcast.485, pred[32,32]{1,0:T(8,128)(4,1)S(1)} %fusion.140, f32[4,8,2,8192]{3,2,1,0:T(2,128)S(1)} %bitcast.470), kind=kOutput, calls=%fused_computation.188 | convolution fusion | flops 202375168 | bytes 6292736 | tf_op jit(solution)/shard_map/dot_general | solution.py:112
  171.4 2.9 copy.205
  174.3 6.4 %all-to-all-start.2 = ((f32[32,2,8192]{2,1,0:T(2,128)}), f32[32,2,8192]{2,1,0:T(2,128)}, u32[]{:S(2)}, u32[]{:S(2)}) async-start(f32[32,2,8192]{2,1,0:T(2,128)} %copy.205), calls=%async_computation.2 | async-start | bytes 4194304 | tf_op jit(solution)/shard_map/all_to_all | solution.py:123
  180.8 5.8 %fusion.129 = f32[2,4,8,8192]{3,2,1,0:T(8,128)S(1)} fusion(f32[32,2,8192]{2,1,0:T(2,128)} %all-to-all-done.3, f32[32,2]{0,1:T(2,128)S(1)} %bitcast.486, s32[32]{0:T(128)S(1)} %copy-done.14, f32[4,8,2,8192]{3,2,1,0:T(2,128)} %bitcast.471), kind=kOutput, calls=%fused_computation.190 | convolution fusion | flops 202376192 | bytes 6291840 | tf_op jit(solution)/shard_map/dot_general | solution.py:101
  187.7 3.0 copy.210
  190.7 39.5 %all-to-all-done.2 = f32[32,2,8192]{2,1,0:T(2,128)} async-done(((f32[32,2,8192]{2,1,0:T(2,128)}), f32[32,2,8192]{2,1,0:T(2,128)}, u32[]{:S(2)}, u32[]{:S(2)}) %all-to-all-start.2) | async-done | bytes 2097184 | tf_op jit(solution)/shard_map/all_to_all | solution.py:123
  230.2 6.4 %all-to-all-start.4 = ((f32[32,2,8192]{2,1,0:T(2,128)}), f32[32,2,8192]{2,1,0:T(2,128)}, u32[]{:S(2)}, u32[]{:S(2)}) async-start(f32[32,2,8192]{2,1,0:T(2,128)} %copy.210), calls=%async_computation.4 | async-start | bytes 4194304 | tf_op jit(solution)/shard_map/all_to_all | solution.py:123
  236.7 4.0 reshape.258
  240.7 45.2 %all-to-all-done.4 = f32[32,2,8192]{2,1,0:T(2,128)} async-done(((f32[32,2,8192]{2,1,0:T(2,128)}), f32[32,2,8192]{2,1,0:T(2,128)}, u32[]{:S(2)}, u32[]{:S(2)}) %all-to-all-start.4) | async-done | bytes 2097184 | tf_op jit(solution)/shard_map/all_to_all | solution.py:123
  286.0 4.1 reshape.260
  290.0 116.3 %while.31 = (s32[]{:T(128)}, bf16[4,256,16,64]{1,3,2,0:T(8,128)(2,1)}, f32[4,16,256]{2,1,0:T(8,128)}, f32[4,256,128]{2,1,0:T(8,128)}, f32[4,256,128]{2,1,0:T(8,1...) while((s32[]{:T(128)}, ...), condition=%wide.region_20.22_spmd, body=%wide.region_5.21_spmd.sunk | while | flops 1289793792 | bytes 13424393 | solution.py:213
  292.2 4.8 %fusion.216 = (f32[16,256]{1,0:T(8,128)S(1)}, f32[16,256]{1,0:T(8,128)S(1)}, f32[16,256]{1,0:T(8,128)}, bf16[256,256]{1,0:T(8,128)(2,1)S(1)}) fusion(f32[16,256]{1,0:T(8,128)S(1)} %get-tuple-element.432, f32[256,256]{1,0:T(8,128)S(1)} %fusion.209, f32[16,256]{1,0:T(8,128)S(1)} %copy_bitcast_fusion.21, pred[256,256]{1,0:T(8,128)(4,1)S(1)} %iota_compare_fusion.4, ...), kind=kOutput, calls=%fused_computation.53.clone.1 | convolution fusion | flops 151965696 | bytes 1606656 | tf_op jit(solution)/shard_map/while/body/eval_jaxpr/transpose(jvp(hts,shp->thp))/dot_general | solution.py:35
  297.1 2.5 reduce-window.52
  299.9 1.5 fusion.210
  301.7 1.6 fusion.211
  305.5 2.5 reduce-window.54
  308.2 1.4 fusion.217
  309.6 3.3 fusion.215
  313.2 2.2 fusion.219
  315.5 3.5 fusion.221
  321.3 4.8 %fusion.216 = (f32[16,256]{1,0:T(8,128)S(1)}, f32[16,256]{1,0:T(8,128)S(1)}, f32[16,256]{1,0:T(8,128)}, bf16[256,256]{1,0:T(8,128)(2,1)S(1)}) fusion(f32[16,256]{1,0:T(8,128)S(1)} %get-tuple-element.432, f32[256,256]{1,0:T(8,128)S(1)} %fusion.209, f32[16,256]{1,0:T(8,128)S(1)} %copy_bitcast_fusion.21, pred[256,256]{1,0:T(8,128)(4,1)S(1)} %iota_compare_fusion.4, ...), kind=kOutput, calls=%fused_computation.53.clone.1 | convolution fusion | flops 151965696 | bytes 1606656 | tf_op jit(solution)/shard_map/while/body/eval_jaxpr/transpose(jvp(hts,shp->thp))/dot_general | solution.py:35
  326.2 2.5 reduce-window.52
  329.0 1.5 fusion.210
  330.8 1.6 fusion.211
  334.6 2.5 reduce-window.54
  337.2 1.4 fusion.217
  338.7 3.3 fusion.215
  342.2 2.2 fusion.219
  344.6 3.5 fusion.221
  350.4 4.8 %fusion.216 = (f32[16,256]{1,0:T(8,128)S(1)}, f32[16,256]{1,0:T(8,128)S(1)}, f32[16,256]{1,0:T(8,128)}, bf16[256,256]{1,0:T(8,128)(2,1)S(1)}) fusion(f32[16,256]{1,0:T(8,128)S(1)} %get-tuple-element.432, f32[256,256]{1,0:T(8,128)S(1)} %fusion.209, f32[16,256]{1,0:T(8,128)S(1)} %copy_bitcast_fusion.21, pred[256,256]{1,0:T(8,128)(4,1)S(1)} %iota_compare_fusion.4, ...), kind=kOutput, calls=%fused_computation.53.clone.1 | convolution fusion | flops 151965696 | bytes 1606656 | tf_op jit(solution)/shard_map/while/body/eval_jaxpr/transpose(jvp(hts,shp->thp))/dot_general | solution.py:35
  355.2 2.5 reduce-window.52
  358.0 1.5 fusion.210
  359.9 1.6 fusion.211
  363.7 2.5 reduce-window.54
  366.3 1.4 fusion.217
  367.7 3.3 fusion.215
  371.3 2.2 fusion.219
  373.7 3.5 fusion.221
  379.5 4.8 %fusion.216 = (f32[16,256]{1,0:T(8,128)S(1)}, f32[16,256]{1,0:T(8,128)S(1)}, f32[16,256]{1,0:T(8,128)}, bf16[256,256]{1,0:T(8,128)(2,1)S(1)}) fusion(f32[16,256]{1,0:T(8,128)S(1)} %get-tuple-element.432, f32[256,256]{1,0:T(8,128)S(1)} %fusion.209, f32[16,256]{1,0:T(8,128)S(1)} %copy_bitcast_fusion.21, pred[256,256]{1,0:T(8,128)(4,1)S(1)} %iota_compare_fusion.4, ...), kind=kOutput, calls=%fused_computation.53.clone.1 | convolution fusion | flops 151965696 | bytes 1606656 | tf_op jit(solution)/shard_map/while/body/eval_jaxpr/transpose(jvp(hts,shp->thp))/dot_general | solution.py:35
  384.3 2.5 reduce-window.52
  387.1 1.5 fusion.210
  388.9 1.6 fusion.211
  392.8 2.5 reduce-window.54
  396.8 3.3 fusion.215
  400.4 2.2 fusion.219
  402.8 3.5 fusion.221
  406.3 1.5 bitcast_reduce_fusion
  409.7 2.8 copy.213
  (282 shorter events, 39.4 us)
Async XLA Ops:
  3.9 4.3 %copy-start.4 = (bf16[1,256,256]{2,1,0:T(8,128)(2,1)S(1)}, bf16[1,256,256]{2,1,0:T(8,128)(2,1)}, u32[]{:S(2)}) copy-start(bf16[1,256,256]{2,1,0:T(8,128)(2,1)} %param.18) | copy-start | bytes 393220
  4.0 4.4 %copy-start.5 = (bf16[1,256,256]{2,1,0:T(8,128)(2,1)S(1)}, bf16[1,256,256]{2,1,0:T(8,128)(2,1)}, u32[]{:S(2)}) copy-start(bf16[1,256,256]{2,1,0:T(8,128)(2,1)} %param.17) | copy-start | bytes 393220
  4.0 4.4 %copy-start.15 = (f32[64]{0:T(128)S(1)}, f32[64]{0:T(128)}, u32[]{:S(2)}) copy-start(f32[64]{0:T(128)} %param.19) | copy-start | bytes 772
  4.0 4.5 %copy-start.16 = (f32[64]{0:T(128)S(1)}, f32[64]{0:T(128)}, u32[]{:S(2)}) copy-start(f32[64]{0:T(128)} %param.20) | copy-start | bytes 772
  4.0 4.7 %copy-start.2 = (f32[1,64,256]{2,1,0:T(8,128)S(1)}, f32[1,64,256]{2,1,0:T(8,128)}, u32[]{:S(2)}) copy-start(f32[1,64,256]{2,1,0:T(8,128)} %param.16) | copy-start | bytes 196612
  28.5 21.0 %all-to-all-start.1 = ((f32[32,2,1]{1,2,0:T(1,128)}), f32[32,2,1]{1,2,0:T(1,128)S(1)}, u32[]{:S(2)}, u32[]{:S(2)}) async-start(f32[32,2,1]{1,2,0:T(1,128)} %bitcast.53), calls=%async_computation.1 | async-start | bytes 32768 | tf_op jit(solution)/shard_map/all_to_all | solution.py:119
  49.6 53.9 %all-to-all-start = ((f32[32,2,8192]{2,1,0:T(2,128)}), f32[32,2,8192]{2,1,0:T(2,128)}, u32[]{:S(2)}, u32[]{:S(2)}) async-start(f32[32,2,8192]{2,1,0:T(2,128)} %all_to_all.26), calls=%async_computation | async-start | bytes 4194304 | tf_op jit(solution)/shard_map/all_to_all | solution.py:119
  57.8 51.9 %copy-start.13 = (s32[32,12]{0,1:T(8,128)S(1)}, s32[32,12]{0,1:T(8,128)}, u32[]{:S(2)}) copy-start(s32[32,12]{0,1:T(8,128)} %param.24) | copy-start | bytes 4612
  103.5 55.6 %all-to-all-start.3 = ((f32[32,2,8192]{2,1,0:T(2,128)}), f32[32,2,8192]{2,1,0:T(2,128)}, u32[]{:S(2)}, u32[]{:S(2)}) async-start(f32[32,2,8192]{2,1,0:T(2,128)} %all_to_all.31), calls=%async_computation.3 | async-start | bytes 4194304 | tf_op jit(solution)/shard_map/all_to_all | solution.py:119
  174.3 6.4 %copy-start.14 = (s32[32]{0:T(128)S(1)}, s32[32]{0:T(128)}, u32[]{:S(2)}) copy-start(s32[32]{0:T(128)} %param.23) | copy-start | bytes 388
  174.3 55.8 %all-to-all-start.2 = ((f32[32,2,8192]{2,1,0:T(2,128)}), f32[32,2,8192]{2,1,0:T(2,128)}, u32[]{:S(2)}, u32[]{:S(2)}) async-start(f32[32,2,8192]{2,1,0:T(2,128)} %copy.205), calls=%async_computation.2 | async-start | bytes 4194304 | tf_op jit(solution)/shard_map/all_to_all | solution.py:123
  190.7 45.9 %copy-start.17 = (f32[64]{0:T(128)S(1)}, f32[64]{0:T(128)}, u32[]{:S(2)}) copy-start(f32[64]{0:T(128)} %param.21) | copy-start | bytes 772
  230.2 55.8 %all-to-all-start.4 = ((f32[32,2,8192]{2,1,0:T(2,128)}), f32[32,2,8192]{2,1,0:T(2,128)}, u32[]{:S(2)}, u32[]{:S(2)}) async-start(f32[32,2,8192]{2,1,0:T(2,128)} %copy.210), calls=%async_computation.4 | async-start | bytes 4194304 | tf_op jit(solution)/shard_map/all_to_all | solution.py:123
  290.0 0.6 copy-start.9
  290.0 0.6 copy-start.11
  290.0 2.2 copy-start.7
  290.5 0.6 copy-start.6
  292.2 4.9 %copy-start = (f32[256,256]{1,0:T(8,128)}, f32[256,256]{1,0:T(8,128)S(1)}, u32[]{:S(2)}) copy-start(f32[256,256]{1,0:T(8,128)S(1)} %fusion.209) | copy-start | bytes 786436 | tf_op jit(solution)/shard_map/while
  309.6 3.6 copy-start.3
  312.9 6.2 %copy-start.8 = (f32[4,16]{1,0:T(4,128)S(1)}, f32[4,16]{1,0:T(4,128)}, u32[]{:S(2)}) copy-start(f32[4,16]{1,0:T(4,128)} %copy-done.7) | copy-start | bytes 772 | tf_op jit(solution)/shard_map/while
  312.9 6.2 %copy-start.10 = (f32[4,16]{1,0:T(4,128)S(1)}, f32[4,16]{1,0:T(4,128)}, u32[]{:S(2)}) copy-start(f32[4,16]{1,0:T(4,128)} %copy-done.9) | copy-start | bytes 772 | tf_op jit(solution)/shard_map/while
  312.9 6.2 %copy-start.12 = (f32[4,16]{1,0:T(4,128)S(1)}, f32[4,16]{1,0:T(4,128)}, u32[]{:S(2)}) copy-start(f32[4,16]{1,0:T(4,128)} %copy-done.11) | copy-start | bytes 772 | tf_op jit(solution)/shard_map/while
  319.1 0.7 copy-start.9
  319.1 0.7 copy-start.11
  319.1 2.2 copy-start.7
  319.6 0.6 copy-start.6
  321.3 4.9 %copy-start = (f32[256,256]{1,0:T(8,128)}, f32[256,256]{1,0:T(8,128)S(1)}, u32[]{:S(2)}) copy-start(f32[256,256]{1,0:T(8,128)S(1)} %fusion.209) | copy-start | bytes 786436 | tf_op jit(solution)/shard_map/while
  338.7 3.6 copy-start.3
  342.0 6.2 %copy-start.8 = (f32[4,16]{1,0:T(4,128)S(1)}, f32[4,16]{1,0:T(4,128)}, u32[]{:S(2)}) copy-start(f32[4,16]{1,0:T(4,128)} %copy-done.7) | copy-start | bytes 772 | tf_op jit(solution)/shard_map/while
  342.0 6.2 %copy-start.10 = (f32[4,16]{1,0:T(4,128)S(1)}, f32[4,16]{1,0:T(4,128)}, u32[]{:S(2)}) copy-start(f32[4,16]{1,0:T(4,128)} %copy-done.9) | copy-start | bytes 772 | tf_op jit(solution)/shard_map/while
  342.0 6.2 %copy-start.12 = (f32[4,16]{1,0:T(4,128)S(1)}, f32[4,16]{1,0:T(4,128)}, u32[]{:S(2)}) copy-start(f32[4,16]{1,0:T(4,128)} %copy-done.11) | copy-start | bytes 772 | tf_op jit(solution)/shard_map/while
  348.2 0.7 copy-start.9
  348.2 0.7 copy-start.11
  348.2 2.2 copy-start.7
  348.7 0.6 copy-start.6
  350.3 4.9 %copy-start = (f32[256,256]{1,0:T(8,128)}, f32[256,256]{1,0:T(8,128)S(1)}, u32[]{:S(2)}) copy-start(f32[256,256]{1,0:T(8,128)S(1)} %fusion.209) | copy-start | bytes 786436 | tf_op jit(solution)/shard_map/while
  367.7 3.6 copy-start.3
  371.1 6.1 %copy-start.8 = (f32[4,16]{1,0:T(4,128)S(1)}, f32[4,16]{1,0:T(4,128)}, u32[]{:S(2)}) copy-start(f32[4,16]{1,0:T(4,128)} %copy-done.7) | copy-start | bytes 772 | tf_op jit(solution)/shard_map/while
  371.1 6.1 %copy-start.10 = (f32[4,16]{1,0:T(4,128)S(1)}, f32[4,16]{1,0:T(4,128)}, u32[]{:S(2)}) copy-start(f32[4,16]{1,0:T(4,128)} %copy-done.9) | copy-start | bytes 772 | tf_op jit(solution)/shard_map/while
  371.1 6.1 %copy-start.12 = (f32[4,16]{1,0:T(4,128)S(1)}, f32[4,16]{1,0:T(4,128)}, u32[]{:S(2)}) copy-start(f32[4,16]{1,0:T(4,128)} %copy-done.11) | copy-start | bytes 772 | tf_op jit(solution)/shard_map/while
  377.2 0.7 copy-start.9
  377.2 0.7 copy-start.11
  377.2 2.2 copy-start.7
  377.8 0.6 copy-start.6
  379.4 4.9 %copy-start = (f32[256,256]{1,0:T(8,128)}, f32[256,256]{1,0:T(8,128)S(1)}, u32[]{:S(2)}) copy-start(f32[256,256]{1,0:T(8,128)S(1)} %fusion.209) | copy-start | bytes 786436 | tf_op jit(solution)/shard_map/while
  396.8 3.6 copy-start.3
  400.1 6.1 %copy-start.8 = (f32[4,16]{1,0:T(4,128)S(1)}, f32[4,16]{1,0:T(4,128)}, u32[]{:S(2)}) copy-start(f32[4,16]{1,0:T(4,128)} %copy-done.7) | copy-start | bytes 772 | tf_op jit(solution)/shard_map/while
  400.1 6.1 %copy-start.10 = (f32[4,16]{1,0:T(4,128)S(1)}, f32[4,16]{1,0:T(4,128)}, u32[]{:S(2)}) copy-start(f32[4,16]{1,0:T(4,128)} %copy-done.9) | copy-start | bytes 772 | tf_op jit(solution)/shard_map/while
  400.1 6.1 %copy-start.12 = (f32[4,16]{1,0:T(4,128)S(1)}, f32[4,16]{1,0:T(4,128)}, u32[]{:S(2)}) copy-start(f32[4,16]{1,0:T(4,128)} %copy-done.11) | copy-start | bytes 772 | tf_op jit(solution)/shard_map/while
  406.3 3.4 copy-start.1
where the time goes:
time: 415 us; the launch traced here: 413 us
  waiting for transfers between devices  186 us (45%)
  matrix products  96.8 us (23%)
  other arithmetic  49.5 us (12%)
  local copies, waits for them, and re-layouts  43.7 us (11%)
  starting transfers between devices  35 us (8%)
    all_to_all x3, waiting for transfers between devices, to_slices(): lax.all_to_all(payload, 'leaf', split_axis=0, concat_axis=0, tiled=True)  101 us
    all_to_all x2, waiting for transfers between devices, to_nodes(): lax.all_to_all(payload, 'leaf', split_axis=0, concat_axis=0, tiled=True)  84.7 us
    dot_general x8, matrix products, intra_terms(): jnp.einsum('hts,shp->thp', mixing, lowered(x_block), preferred_element_ty...  32.6 us
    another operation x44, other arithmetic  25.8 us
    all_to_all x3, starting transfers between devices, to_slices(): lax.all_to_all(payload, 'leaf', split_axis=0, concat_axis=0, tiled=True)  22.3 us
    dot_general x8, matrix products, state_terms(): jnp.einsum('tn,hpn->thp', c_block, start_block, precision=highest)  20.6 us
    dot_general x8, matrix products, state_terms(): jnp.einsum('shp,sn->hpn', weighted, lowered(b_block), preferred_element_t...  14.9 us
    all_to_all x2, starting transfers between devices, to_nodes(): lax.all_to_all(payload, 'leaf', split_axis=0, concat_axis=0, tiled=True)  12.8 us
  transfers between devices with their start and end apart: 5, of which 5 were waited for; matrix products, arithmetic and copies ran while one was open for 3% of the time, Pallas kernels for 0%

commit v1 on v0

v1 whole, which is shorter than its diff:
```python
import functools

import jax
import jax.numpy as jnp
from jax import lax
from jax.experimental import pallas as pl
from jax.experimental.pallas import tpu as pltpu
from jax.sharding import PartitionSpec as P

HEAD_DIM = 64
STATE = 128
BLOCK = 8
TREE_DEPTH = 3
F32 = jnp.float32
BF16 = jnp.bfloat16

highest = lax.Precision.HIGHEST


def dot(a, b, da=1, db=0):
    return lax.dot_general(a, b, (((da,), (db,)), ((), ())), preferred_element_type=F32)


def prefix(rows, ones):
    top = rows.astype(BF16)
    rest = rows - top.astype(F32)
    mid = rest.astype(BF16)
    low = (rest - mid.astype(F32)).astype(BF16)
    return dot(top, ones) + (dot(mid, ones) + dot(low, ones))


def triangle(n, lower):
    r = lax.broadcasted_iota(jnp.int32, (n, n), 0)
    c = lax.broadcasted_iota(jnp.int32, (n, n), 1)
    return jnp.where(r >= c if lower else r <= c, 1.0, 0.0).astype(BF16)


def rates(raw, alog, bias):
    v = raw + bias
    rate = jnp.maximum(v, 0.0) + jnp.log1p(jnp.exp(-jnp.abs(v)))
    cum = prefix(-jnp.exp(alog) * rate, triangle(raw.shape[1], False))
    return rate, cum


def spread(rows, flat):
    h, t = rows.shape
    return (flat.astype(F32).reshape(h, -1, t) * rows[:, None, :]).reshape(flat.shape)


def fold(flat, heads):
    return flat.reshape(heads, -1, flat.shape[1]).sum(axis=1)


def first_kernel(x_ref, dy_ref, raw_ref, b_ref, c_ref, alog_ref, bias_ref, end_ref, pull_ref, carry_ref, xt_ref, dyt_ref):
    rate, cum = rates(raw_ref[...], alog_ref[...], bias_ref[...])
    last = cum[:, -1:]
    tail = jnp.exp(last - cum) * rate
    growth = jnp.exp(cum)
    xt = x_ref[...].T
    dyt = dy_ref[...].T
    xt_ref[...] = xt
    dyt_ref[...] = dyt
    end_ref[...] = dot(spread(tail, xt).astype(BF16), b_ref[...])
    pull_ref[...] = dot(spread(growth, dyt).astype(BF16), c_ref[...])
    carry_ref[...] = jnp.broadcast_to(jnp.exp(last), carry_ref.shape)


def inner_kernel(per, dy_ref, raw_ref, b_ref, c_ref, alog_ref, bias_ref, skip_ref, xt_ref, dyt_ref, dx_ref, row_ref, col_ref, dbt_ref, dct_ref, score, total):
    t = raw_ref.shape[1]
    half = t // 2
    step = pl.program_id(0)

    @pl.when(step % per == 0)
    def _():
        score[...] = dot(c_ref[...], b_ref[...], 1, 1)
        total[...] = jnp.zeros_like(total)

    rate, cum = rates(raw_ref[...], alog_ref[...], bias_ref[...])
    rowterm = jnp.log(rate) - cum
    cumt = cum.T
    r = lax.broadcasted_iota(jnp.int32, (half, half), 0)
    c = lax.broadcasted_iota(jnp.int32, (half, half), 1)
    causal = r >= c
    lane = lax.broadcasted_iota(jnp.int32, (2 * HEAD_DIM, t), 0)
    lefts = []
    for i in range(BLOCK):
        pair = slice(i // 2 * 2 * HEAD_DIM, (i // 2 + 1) * 2 * HEAD_DIM)
        mine = slice(i * HEAD_DIM, (i + 1) * HEAD_DIM)
        xpair = xt_ref[pair, :]
        xhead = jnp.where((lane // HEAD_DIM) == i % 2, xpair, jnp.zeros_like(xpair))
        dyh = dyt_ref[mine, :]
        skip = skip_ref[i:i + 1, :]
        parts = {}
        for a, b in ((0, 0), (1, 0), (1, 1)):
            rows = slice(a * half, (a + 1) * half)
            cols = slice(b * half, (b + 1) * half)
            gap = cumt[rows, i:i + 1] + rowterm[i:i + 1, cols]
            if a == b:
                gap = jnp.where(causal, gap, -1e30)
            decay = jnp.exp(gap)
            mix = decay * score[rows, cols]
            dmix = dot(dy_ref[rows, pair], xhead[:, cols])
            total[rows, cols] += dmix * decay
            parts[a, b] = (mix.astype(BF16), dmix * mix)
        q0, q1, q2 = parts[0, 0][1], parts[1, 0][1], parts[1, 1][1]
        col_ref[i:i + 1, :half] = jnp.sum(q0 + q1, axis=0, keepdims=True)
        col_ref[i:i + 1, half:] = jnp.sum(q2, axis=0, keepdims=True)
        lefts.append(jnp.concatenate([jnp.sum(q0, axis=1, keepdims=True), jnp.sum(q1 + q2, axis=1, keepdims=True)], axis=0))
        left = jnp.concatenate([parts[0, 0][0], parts[1, 0][0]], axis=0)
        dx_ref[mine, :half] = dot(dyh, left) + skip * dyh[:, :half].astype(F32)
        dx_ref[mine, half:] = dot(dyh[:, half:], parts[1, 1][0]) + skip * dyh[:, half:].astype(F32)
    row_ref[...] = jnp.concatenate(lefts, axis=1).T

    @pl.when(step % per == per - 1)
    def _():
        summed = jnp.where(
            lax.broadcasted_iota(jnp.int32, (t, t), 0) >= lax.broadcasted_iota(jnp.int32, (t, t), 1), total[...], 0.0
        ).astype(BF16)
        dbt_ref[...] = dot(c_ref[...], summed, 0, 0)
        dct_ref[...] = dot(b_ref[...], summed, 0, 1)


def last_kernel(per, raw_ref, b_ref, c_ref, alog_ref, bias_ref, xt_ref, dyt_ref, start_ref, grad_ref, dx_ref, row_ref, col_ref, dbt_ref, dct_ref, gx_ref, gdt_ref, gb_ref, gc_ref, sumb, sumc):
    step = pl.program_id(0)
    t = raw_ref.shape[1]

    @pl.when(step % per == 0)
    def _():
        sumb[...] = dbt_ref[...]
        sumc[...] = dct_ref[...]

    v = raw_ref[...] + bias_ref[...]
    rate, cum = rates(raw_ref[...], alog_ref[...], bias_ref[...])
    last = cum[:, -1:]
    growth = jnp.exp(cum)
    tail = jnp.exp(last - cum) * rate
    start = start_ref[...]
    grad = grad_ref[...]
    inner = jnp.sum(fold(start * grad, BLOCK), axis=1, keepdims=True)
    start_low = start.astype(BF16)
    grad_low = grad.astype(BF16)
    xt = xt_ref[...]
    dyt = dyt_ref[...]
    pulled = dot(grad_low, b_ref[...], 1, 1)
    z = fold(xt.astype(F32) * pulled, BLOCK) * tail
    gx_ref[...] = (dx_ref[...] + spread(tail, pulled)).astype(BF16).T
    sumb[...] += dot(grad_low, spread(tail, xt).astype(BF16), 0, 0)
    carried = dot(start_low, c_ref[...], 1, 1)
    g = fold(dyt.astype(F32) * carried, BLOCK) * growth
    sumc[...] += dot(start_low, spread(growth, dyt).astype(BF16), 0, 0)
    col = col_ref[...]
    dcum = row_ref[...] - col + g - z
    at_end = jnp.sum(z, axis=1, keepdims=True) + growth[:, -1:] * inner
    dlog = prefix(dcum, triangle(t, True)) + at_end
    slope = 1.0 / (1.0 + jnp.exp(-v))
    gdt_ref[...] = ((col + z) / rate - jnp.exp(alog_ref[...]) * dlog) * slope

    @pl.when(step % per == per - 1)
    def _():
        gb_ref[...] = sumb[...].T
        gc_ref[...] = sumc[...].T


def specs(per, t):
    flat = pl.BlockSpec((BLOCK * HEAD_DIM, t), lambda i: (i, 0))
    return {
        "nat": pl.BlockSpec((t, BLOCK * HEAD_DIM), lambda i: (0, i)),
        "rows": pl.BlockSpec((BLOCK, t), lambda i: (i, 0)),
        "group": pl.BlockSpec((t, STATE), lambda i: (0, i // per)),
        "one": pl.BlockSpec((BLOCK, 1), lambda i: (i, 0)),
        "flat": flat,
        "state": pl.BlockSpec((BLOCK * HEAD_DIM, STATE), lambda i: (i, 0)),
        "lane": pl.BlockSpec((BLOCK, STATE), lambda i: (i, 0)),
        "groupt": pl.BlockSpec((STATE, t), lambda i: (i // per, 0)),
    }


def params(mib):
    return pltpu.CompilerParams(vmem_limit_bytes=mib << 20)


def sds(shape, kind=F32):
    return jax.ShapeDtypeStruct(shape, kind)


def summaries(x, dy, raw, b, c, alog, bias, per):
    heads, t = raw.shape
    s = specs(per, t)
    return pl.pallas_call(
        first_kernel,
        grid=(heads // BLOCK,),
        in_specs=[s["nat"], s["nat"], s["rows"], s["group"], s["group"], s["one"], s["one"]],
        out_specs=[s["state"], s["state"], s["lane"], s["flat"], s["flat"]],
        out_shape=[
            sds((heads * HEAD_DIM, STATE)),
            sds((heads * HEAD_DIM, STATE)),
            sds((heads, STATE)),
            sds((heads * HEAD_DIM, t), BF16),
            sds((heads * HEAD_DIM, t), BF16),
        ],
        compiler_params=params(32),
        name="summaries",
    )(x, dy, raw, b, c, alog, bias)


def inner_grads(dy, raw, b, c, alog, bias, skip, xt, dyt, per):
    heads, t = raw.shape
    s = specs(per, t)
    groups = heads // BLOCK // per
    return pl.pallas_call(
        functools.partial(inner_kernel, per),
        grid=(heads // BLOCK,),
        in_specs=[s["nat"], s["rows"], s["group"], s["group"], s["one"], s["one"], s["one"], s["flat"], s["flat"]],
        out_specs=[s["flat"], s["rows"], s["rows"], s["groupt"], s["groupt"]],
        out_shape=[
            sds((heads * HEAD_DIM, t)),
            sds((heads, t)),
            sds((heads, t)),
            sds((groups * STATE, t)),
            sds((groups * STATE, t)),
        ],
        scratch_shapes=[pltpu.VMEM((t, t), F32), pltpu.VMEM((t, t), F32)],
        compiler_params=params(32),
        cost_estimate=pl.CostEstimate(flops=heads * t * t * 256, bytes_accessed=heads * t * 512, transcendentals=heads * t * t),
        name="inner_grads",
    )(dy, raw, b, c, alog, bias, skip, xt, dyt)


def final_grads(raw, b, c, alog, bias, xt, dyt, start, grad, inner, per):
    heads, t = raw.shape
    s = specs(per, t)
    groups = heads // BLOCK // per
    return pl.pallas_call(
        functools.partial(last_kernel, per),
        grid=(heads // BLOCK,),
        in_specs=[s["rows"], s["group"], s["group"], s["one"], s["one"], s["flat"], s["flat"], s["state"], s["state"], s["flat"], s["rows"], s["rows"], s["groupt"], s["groupt"]],
        out_specs=[s["nat"], s["rows"], s["group"], s["group"]],
        out_shape=[
            sds((t, heads * HEAD_DIM), BF16),
            sds((heads, t)),
            sds((t, groups * STATE)),
            sds((t, groups * STATE)),
        ],
        scratch_shapes=[pltpu.VMEM((STATE, t), F32), pltpu.VMEM((STATE, t), F32)],
        compiler_params=params(32),
        name="final_grads",
    )(raw, b, c, alog, bias, xt, dyt, start, grad, *inner)


def forward_tree(own_end, carries, link_up):
    node_count = own_end.shape[0]
    start_state = jnp.zeros_like(own_end)
    for depth_step in range(TREE_DEPTH - 1):
        finish = carries * start_state + own_end
        start_state = jnp.dot(link_up, finish.reshape(node_count, -1), precision=highest).reshape(own_end.shape)
    return start_state


def backward_tree(own_pull, carries, link_down):
    node_count = own_pull.shape[0]
    end_grad = jnp.zeros_like(own_pull)
    for depth_step in range(TREE_DEPTH - 1):
        start_grad = own_pull + carries * end_grad
        end_grad = jnp.dot(link_down, start_grad.reshape(node_count, -1), precision=highest).reshape(own_pull.shape)
    return end_grad


def exchange(payload):
    return lax.all_to_all(payload, "leaf", split_axis=0, concat_axis=0, tiled=True)


def body(inputs, dt_raw, b_proj, c_proj, a_log, dt_bias, skip, grad_out, parent, children):
    heads = a_log.shape[0]
    groups = b_proj.shape[2] // STATE
    per = heads // BLOCK // groups
    nodes = parent.shape[0]
    x, dy, raw, b, c = inputs[0], grad_out[0], dt_raw[0], b_proj[0], c_proj[0]
    alog, bias, skips = a_log[:, None], dt_bias[:, None], skip[:, None]
    own_end, own_pull, carry, xt, dyt = summaries(x, dy, raw, b, c, alog, bias, per)
    node_ids = jnp.arange(nodes, dtype=jnp.int32)
    link_up = (parent[:, None] == node_ids[None, :]).astype(F32)
    link_down = jnp.any(children[:, :, None] == node_ids[None, None, :], axis=1).astype(F32)

    share = heads // nodes

    def as_slices(flat):
        return flat.reshape(nodes, share * HEAD_DIM, STATE)

    carry_slices = jnp.repeat(exchange(carry).reshape(nodes, share, STATE), HEAD_DIM, axis=1)
    start_slices = forward_tree(as_slices(exchange(own_end)), carry_slices, link_up)
    start = exchange(start_slices.reshape(heads * HEAD_DIM, STATE))
    inner = inner_grads(dy, raw, b, c, alog, bias, skips, xt, dyt, per)
    grad_slices = backward_tree(as_slices(exchange(own_pull)), carry_slices, link_down)
    grad = exchange(grad_slices.reshape(heads * HEAD_DIM, STATE))
    gx, gdt, gb, gc = final_grads(raw, b, c, alog, bias, xt, dyt, start, grad, inner, per)
    return gx[None], gdt[None], gb[None], gc[None]


def solution(mesh):
    placed = (
        P(("dp", "leaf"), None, "heads"),
        P(("dp", "leaf"), "heads", None),
        P(("dp", "leaf"), None, "heads"),
        P(("dp", "leaf"), None, "heads"),
        P("heads"),
        P("heads"),
        P("heads"),
        P(("dp", "leaf"), None, "heads"),
        P("dp"),
        P("dp", None),
    )
    return jax.shard_map(
        body,
        mesh=mesh,
        in_specs=placed,
        out_specs=(
            P(("dp", "leaf"), None, "heads"),
            P(("dp", "leaf"), "heads", None),
            P(("dp", "leaf"), None, "heads"),
            P(("dp", "leaf"), None, "heads"),
        ),
        check_vma=False,
    )
```

time: 415 us -> 283 us (0.68)
  matrix products: 96.8 us -> 9.35 us
  blocking collectives: 0 us -> 74.1 us
  waiting for transfers between devices: 186 us -> 116 us
  other arithmetic: 49.5 us -> 7.38 us
  Pallas kernels: 0 us -> 32.8 us
  local copies, waits for them, and re-layouts: 43.7 us -> 24.7 us
  starting transfers between devices: 35 us -> 17.2 us
    dot_general x44 -> x0, matrix products: 83.5 us -> none  [the longest x8 32.6 us: intra_terms(): jnp.einsum('hts,shp->thp', mixing, lowered(x_block), preferred_element_ty...]
    all_to_all x0 -> x2, blocking collectives: none -> 74.1 us  [exchange(): lax.all_to_all(payload, 'leaf', split_axis=0, concat_axis=0, tiled=True)]
    all_to_all x5 -> x3, waiting for transfers between devices: 186 us -> 116 us  [exchange(): lax.all_to_all(payload, 'leaf', split_axis=0, concat_axis=0, tiled=True)]
    pallas_call x0 -> x3, Pallas kernels: none -> 32.8 us  [the longest x1 16.9 us: inner_grads(): pl.pallas_call(functools.partial(inner_kernel, per), grid=(heads // BLOCK...]
    another operation x44 -> x0, other arithmetic: 25.8 us -> none
    all_to_all x5 -> x3, starting transfers between devices: 35 us -> 17.2 us  [exchange(): lax.all_to_all(payload, 'leaf', split_axis=0, concat_axis=0, tiled=True)]
    reshape x9 -> x0, local copies, waits for them, and re-layouts: 8.66 us -> none  [the longest x1 4.05 us: body(): start_blocks = start_state.reshape(blocks, H_BLOCK, HEAD_DIM, STATE)]
    reduce_sum x9 -> x0, other arithmetic: 7.89 us -> none  [the longest x4 5.66 us: state_terms(): growth[:, -1][:, None, None] * start_block]
  transfers between devices with their start and end apart: 5 -> 3, of which waited for: 5 -> 3; matrix products, arithmetic and copies ran while one was open for 3% -> 3% of each run, Pallas kernels for 0% -> 6%
where the time goes in v1:
time: 283 us; the launch traced here: 282 us
  waiting for transfers between devices  116 us (41%)
  blocking collectives  74.1 us (26%)
  Pallas kernels  32.8 us (12%)
  local copies, waits for them, and re-layouts  24.7 us (9%)
  starting transfers between devices  17.2 us (6%)
  matrix products  9.35 us (3%)
  other arithmetic  7.38 us (3%)
    all_to_all x3, waiting for transfers between devices, exchange(): lax.all_to_all(payload, 'leaf', split_axis=0, concat_axis=0, tiled=True)  116 us
    all_to_all x2, blocking collectives, exchange(): lax.all_to_all(payload, 'leaf', split_axis=0, concat_axis=0, tiled=True)  74.1 us
    unnamed x40, local copies, waits for them, and re-layouts  17.9 us
    all_to_all x3, starting transfers between devices, exchange(): lax.all_to_all(payload, 'leaf', split_axis=0, concat_axis=0, tiled=True)  17.2 us
    pallas_call x1, Pallas kernels, inner_grads(): pl.pallas_call(functools.partial(inner_kernel, per), grid=(heads // BLOCK...  16.9 us
    pallas_call x1, Pallas kernels, final_grads(): pl.pallas_call(functools.partial(last_kernel, per), grid=(heads // BLOCK,...  9.16 us
    unnamed x1, other arithmetic  7.24 us
    pallas_call x1, Pallas kernels, summaries(): pl.pallas_call(first_kernel, grid=(heads // BLOCK,), in_specs=[s['nat'],...  6.66 us
  transfers between devices with their start and end apart: 3, of which 3 were waited for; matrix products, arithmetic and copies ran while one was open for 3% of the time, Pallas kernels for 6%

profile of v1, /device:TPU:16, one launch (start us, length us, event | category | flops | bytes accessed | tf_op | source)
XLA Modules:
  0.0 282.4 jit_solution(17192953554500932333)
XLA Ops:
  0.6 0.7 copy.83.alog_ref
  1.4 0.7 copy.84.bias_ref
  2.1 0.0 copy-start.2
  2.1 1.6 copy-done.2
  3.7 0.0 copy-start.3
  3.7 1.6 copy-done.3
  5.3 0.0 copy-start.11
  5.3 0.9 copy-done.11
  6.2 0.0 copy-start.13
  6.2 0.9 copy-done.13
  7.1 0.0 copy-start.15
  7.1 0.8 copy-done.15
  8.0 6.7 %summaries.1 = (f32[4096,128]{1,0:T(8,128)S(1)}, f32[4096,128]{1,0:T(8,128)}, f32[64,128]{1,0:T(8,128)S(1)}, bf16[4096,256]{1,0:T(8,128)(2,1)S(1)}, bf16[4096,256]{1,0:T(8,128)(2,1)S(1)}) custom-call(bf16[256,4096]{1,0:T(8,128)(2,1)S(1)} %bitcast.101, bf16[256,4096]{1,0:T(8,128)(2,1)S(1)} %bitcast.102, f32[64,256]{1,0:T(8,128)S(1)} %bitcast.111, ...), custom_call_target="tpu_custom_call" | custom-call | tf_op jit(solution)/shard_map/summaries/pallas_call | solution.py:189
  14.6 0.0 copy-start.5
  14.6 0.0 copy-start.8
  14.6 21.0 %all_to_all.43 = f32[32,2,128]{2,1,0:T(2,128)S(1)} all-to-all(f32[32,2,128]{2,1,0:T(2,128)S(1)} %bitcast.114), channel_id=1, replica_groups=mesh['leaf'=32,'heads'=2,'dp'=4] {'leaf'}, dimensions={0} | all-to-all | bytes 65536 | tf_op jit(solution)/shard_map/all_to_all | solution.py:269
  35.6 53.0 %all_to_all.44 = f32[32,128,128]{2,1,0:T(8,128)S(1)} all-to-all(f32[32,128,128]{2,1,0:T(8,128)S(1)} %bitcast.104), channel_id=1, replica_groups=mesh['leaf'=32,'heads'=2,'dp'=4] {'leaf'}, dimensions={0} | all-to-all | bytes 4194304 | tf_op jit(solution)/shard_map/all_to_all | solution.py:269
  88.7 0.0 copy-done.5
  88.7 0.0 copy-done.8
  88.7 5.1 %all-to-all-start.3 = ((f32[32,128,128]{2,1,0:T(8,128)}), f32[32,128,128]{2,1,0:T(8,128)}, u32[]{:S(2)}, u32[]{:S(2)}) async-start(f32[32,128,128]{2,1,0:T(8,128)} %bitcast.15), calls=%async_computation.3 | async-start | bytes 4194304 | tf_op jit(solution)/shard_map/all_to_all | solution.py:269
  93.9 49.1 %all-to-all-done.3 = f32[32,128,128]{2,1,0:T(8,128)} async-done(((f32[32,128,128]{2,1,0:T(8,128)}), f32[32,128,128]{2,1,0:T(8,128)}, u32[]{:S(2)}, u32[]{:S(2)}) %all-to-all-start.3) | async-done | bytes 2097184 | tf_op jit(solution)/shard_map/all_to_all | solution.py:269
  143.0 0.1 broadcast_in_dim.33
  143.1 0.0 copy-start.18
  143.1 7.2 %fusion.2 = (f32[4,128,8,128]{3,2,1,0:T(8,128)}, f32[4,128,8,128]{3,2,1,0:T(8,128)S(1)}) fusion(f32[4,8,128,128]{3,2,1,0:T(8,128)} %bitcast.41, f32[4,8,128,128]{3,2,1,0:T(8,128)S(1)} %bitcast.116, f32[4,8,128,128]{3,2,1,0:T(8,128)S(1)} %bitcast.115), kind=kLoop, calls=%fused_computation.5 | loop fusion | flops 1048576 | bytes 10485760
  150.4 0.0 copy-done.18
  150.4 2.4 fusion.23
  152.8 1.2 fusion.10
  154.0 2.5 copy.74
  156.5 0.0 copy-start.17
  156.5 6.0 %all-to-all-start.2 = ((f32[32,128,128]{2,1,0:T(8,128)}), f32[32,128,128]{2,1,0:T(8,128)S(1)}, u32[]{:S(2)}, u32[]{:S(2)}) async-start(f32[32,128,128]{2,1,0:T(8,128)} %copy.74), calls=%async_computation.2 | async-start | bytes 4194304 | tf_op jit(solution)/shard_map/all_to_all | solution.py:269
  162.5 0.0 copy-done.17
  162.5 0.1 fusion.26
  162.7 4.6 %fusion.20 = f32[128,4,8,128]{3,2,1,0:T(8,128)S(1)} fusion(f32[4,128,8,128]{3,2,1,0:T(8,128)} %get-tuple-element.32, f32[32,128,128]{2,1,0:T(8,128)} %all-to-all-done.3, f32[32,2,128]{2,0,1:T(8,128)S(1)} %copy.69, pred[32,32]{1,0:T(8,128)(4,1)S(1)} %fusion.26), kind=kOutput, calls=%fused_computation.22 | convolution fusion | flops 202375168 | bytes 6325248 | tf_op jit(solution)/shard_map/dot_general | solution.py:264
  167.3 1.2 fusion.4
  168.4 2.5 copy.79
  171.0 0.0 copy-start.19
  171.0 0.0 copy-start.12
  171.0 0.0 copy-start.14
  171.0 0.0 copy-start.16
  171.0 41.2 %all-to-all-done.2 = f32[32,128,128]{2,1,0:T(8,128)S(1)} async-done(((f32[32,128,128]{2,1,0:T(8,128)}), f32[32,128,128]{2,1,0:T(8,128)S(1)}, u32[]{:S(2)}, u32[]{:S(2)}) %all-to-all-start.2) | async-done | bytes 2097184 | tf_op jit(solution)/shard_map/all_to_all | solution.py:269
  212.1 6.1 %all-to-all-start.4 = ((f32[32,128,128]{2,1,0:T(8,128)}), f32[32,128,128]{2,1,0:T(8,128)}, u32[]{:S(2)}, u32[]{:S(2)}) async-start(f32[32,128,128]{2,1,0:T(8,128)} %copy.79), calls=%async_computation.4 | async-start | bytes 4194304 | tf_op jit(solution)/shard_map/all_to_all | solution.py:269
  218.2 0.0 copy-done.19
  218.2 0.1 copy.82.skip_ref
  218.3 0.0 copy-done.12
  218.3 0.0 copy-done.14
  218.3 0.0 copy-done.16
  218.3 0.0 copy-start.4
  218.4 1.6 copy-done.4
  219.9 0.0 copy-start.6
  219.9 1.6 copy-done.6
  221.5 0.0 copy-start.9
  221.5 1.6 copy-done.9
  223.1 16.9 %inner_grads.1 = (f32[4096,256]{1,0:T(8,128)S(1)}, f32[64,256]{1,0:T(8,128)S(1)}, f32[64,256]{1,0:T(8,128)S(1)}, f32[256,256]{1,0:T(8,128)S(1)}, f32[256,256]{1,0:T(8,128)S(1)}) custom-call(bf16[256,4096]{1,0:T(8,128)(2,1)S(1)} %bitcast.103, f32[64,256]{1,0:T(8,128)S(1)} %bitcast.112, bf16[256,256]{1,0:T(8,128)(2,1)S(1)} %bitcast.106, ...), custom_call_target="tpu_custom_call" | custom-call | flops 1073741824 | bytes 8388608 | tf_op jit(solution)/shard_map/inner_grads/pallas_call | solution.py:210
  240.1 0.0 copy-start
  240.1 1.9 copy-done
  242.0 25.8 %all-to-all-done.4 = f32[32,128,128]{2,1,0:T(8,128)} async-done(((f32[32,128,128]{2,1,0:T(8,128)}), f32[32,128,128]{2,1,0:T(8,128)}, u32[]{:S(2)}, u32[]{:S(2)}) %all-to-all-start.4) | async-done | bytes 2097184 | tf_op jit(solution)/shard_map/all_to_all | solution.py:269
  267.9 0.0 copy-start.1
  267.9 2.2 copy-done.1
  270.0 0.0 copy-start.7
  270.1 1.6 copy-done.7
  271.6 0.0 copy-start.10
  271.6 1.6 copy-done.10
  273.2 9.2 %final_grads.1 = (bf16[256,4096]{1,0:T(8,128)(2,1)}, f32[64,256]{1,0:T(8,128)}, f32[256,256]{1,0:T(8,128)}, f32[256,256]{1,0:T(8,128)}) custom-call(f32[64,256]{1,0:T(8,128)S(1)} %bitcast.113, bf16[256,256]{1,0:T(8,128)(2,1)S(1)} %bitcast.107, bf16[256,256]{1,0:T(8,128)(2,1)S(1)} %bitcast.110, f32[64,1]{1,0:T(8,128)S(1)} %copy.83.alog_ref, ...), custom_call_target="tpu_custom_call" | custom-call | tf_op jit(solution)/shard_map/final_grads/pallas_call | solution.py:233
  (2 shorter events, 0.0 us)
Async XLA Ops:
  2.1 1.6 copy-start.2
  3.7 1.6 copy-start.3
  5.3 0.9 copy-start.11
  6.2 0.9 copy-start.13
  7.1 0.8 copy-start.15
  14.6 74.1 %copy-start.5 = (bf16[4096,256]{1,0:T(8,128)(2,1)}, bf16[4096,256]{1,0:T(8,128)(2,1)S(1)}, u32[]{:S(2)}) copy-start(bf16[4096,256]{1,0:T(8,128)(2,1)S(1)} %get-tuple-element.18.xt_ref) | copy-start | bytes 6291460
  14.6 74.1 %copy-start.8 = (bf16[4096,256]{1,0:T(8,128)(2,1)}, bf16[4096,256]{1,0:T(8,128)(2,1)S(1)}, u32[]{:S(2)}) copy-start(bf16[4096,256]{1,0:T(8,128)(2,1)S(1)} %get-tuple-element.19.dyt_ref) | copy-start | bytes 6291460
  88.7 54.3 %all-to-all-start.3 = ((f32[32,128,128]{2,1,0:T(8,128)}), f32[32,128,128]{2,1,0:T(8,128)}, u32[]{:S(2)}, u32[]{:S(2)}) async-start(f32[32,128,128]{2,1,0:T(8,128)} %bitcast.15), calls=%async_computation.3 | async-start | bytes 4194304 | tf_op jit(solution)/shard_map/all_to_all | solution.py:269
  143.1 7.3 %copy-start.18 = (s32[32]{0:T(128)S(1)}, s32[32]{0:T(128)}, u32[]{:S(2)}) copy-start(s32[32]{0:T(128)} %param.18) | copy-start | bytes 388
  156.5 6.0 %copy-start.17 = (s32[32,12]{0,1:T(8,128)S(1)}, s32[32,12]{0,1:T(8,128)}, u32[]{:S(2)}) copy-start(s32[32,12]{0,1:T(8,128)} %param.19) | copy-start | bytes 4612
  156.5 55.7 %all-to-all-start.2 = ((f32[32,128,128]{2,1,0:T(8,128)}), f32[32,128,128]{2,1,0:T(8,128)S(1)}, u32[]{:S(2)}, u32[]{:S(2)}) async-start(f32[32,128,128]{2,1,0:T(8,128)} %copy.74), calls=%async_computation.2 | async-start | bytes 4194304 | tf_op jit(solution)/shard_map/all_to_all | solution.py:269
  171.0 47.2 %copy-start.19 = (f32[64]{0:T(128)S(1)}, f32[64]{0:T(128)}, u32[]{:S(2)}) copy-start(f32[64]{0:T(128)} %param.16) | copy-start | bytes 772
  171.0 47.3 %copy-start.12 = (bf16[1,256,256]{2,1,0:T(8,128)(2,1)S(1)}, bf16[1,256,256]{2,1,0:T(8,128)(2,1)}, u32[]{:S(2)}) copy-start(bf16[1,256,256]{2,1,0:T(8,128)(2,1)} %param.12) | copy-start | bytes 393220
  171.0 47.3 %copy-start.14 = (bf16[1,256,256]{2,1,0:T(8,128)(2,1)S(1)}, bf16[1,256,256]{2,1,0:T(8,128)(2,1)}, u32[]{:S(2)}) copy-start(bf16[1,256,256]{2,1,0:T(8,128)(2,1)} %param.13) | copy-start | bytes 393220
  171.0 47.3 %copy-start.16 = (f32[1,64,256]{2,1,0:T(8,128)S(1)}, f32[1,64,256]{2,1,0:T(8,128)}, u32[]{:S(2)}) copy-start(f32[1,64,256]{2,1,0:T(8,128)} %param.11) | copy-start | bytes 196612
  212.1 55.7 %all-to-all-start.4 = ((f32[32,128,128]{2,1,0:T(8,128)}), f32[32,128,128]{2,1,0:T(8,128)}, u32[]{:S(2)}, u32[]{:S(2)}) async-start(f32[32,128,128]{2,1,0:T(8,128)} %copy.79), calls=%async_computation.4 | async-start | bytes 4194304 | tf_op jit(solution)/shard_map/all_to_all | solution.py:269
  218.3 1.6 copy-start.4
  219.9 1.6 copy-start.6
  221.5 1.6 copy-start.9
  240.1 2.0 copy-start
  267.9 2.2 copy-start.1
  270.0 1.6 copy-start.7
  271.6 1.6 copy-start.10

commit v2 on v1

--- a/solution.py
+++ b/solution.py
@@ -10,11 +10,14 @@
 HEAD_DIM = 64
 STATE = 128
 BLOCK = 8
-TREE_DEPTH = 3
+NX = 4
+NZ = 8
+ARM = 4
+LAG = 2
 F32 = jnp.float32
 BF16 = jnp.bfloat16
 
-highest = lax.Precision.HIGHEST
+MESH = pl.DeviceIdType.MESH
 
 
 def dot(a, b, da=1, db=0):
@@ -51,7 +54,7 @@
     return flat.reshape(heads, -1, flat.shape[1]).sum(axis=1)
 
 
-def first_kernel(x_ref, dy_ref, raw_ref, b_ref, c_ref, alog_ref, bias_ref, end_ref, pull_ref, carry_ref, xt_ref, dyt_ref):
+def first_kernel(x_ref, dy_ref, raw_ref, b_ref, c_ref, alog_ref, bias_ref, own_ref, carry_ref, xt_ref, dyt_ref):
     rate, cum = rates(raw_ref[...], alog_ref[...], bias_ref[...])
     last = cum[:, -1:]
     tail = jnp.exp(last - cum) * rate
@@ -60,8 +63,10 @@
     dyt = dy_ref[...].T
     xt_ref[...] = xt
     dyt_ref[...] = dyt
-    end_ref[...] = dot(spread(tail, xt).astype(BF16), b_ref[...])
-    pull_ref[...] = dot(spread(growth, dyt).astype(BF16), c_ref[...])
+    end = dot(spread(tail, xt).astype(BF16), b_ref[...])
+    pull = dot(spread(growth, dyt).astype(BF16), c_ref[...])
+    own_ref[:, 0] = end.reshape(BLOCK, HEAD_DIM, STATE)
+    own_ref[:, 1] = pull.reshape(BLOCK, HEAD_DIM, STATE)
     carry_ref[...] = jnp.broadcast_to(jnp.exp(last), carry_ref.shape)
 
 
@@ -120,7 +125,7 @@
         dct_ref[...] = dot(b_ref[...], summed, 0, 1)
 
 
-def last_kernel(per, raw_ref, b_ref, c_ref, alog_ref, bias_ref, xt_ref, dyt_ref, start_ref, grad_ref, dx_ref, row_ref, col_ref, dbt_ref, dct_ref, gx_ref, gdt_ref, gb_ref, gc_ref, sumb, sumc):
+def last_kernel(per, raw_ref, b_ref, c_ref, alog_ref, bias_ref, xt_ref, dyt_ref, both_ref, dx_ref, row_ref, col_ref, dbt_ref, dct_ref, gx_ref, gdt_ref, gb_ref, gc_ref, sumb, sumc):
     step = pl.program_id(0)
     t = raw_ref.shape[1]
 
@@ -134,8 +139,8 @@
     last = cum[:, -1:]
     growth = jnp.exp(cum)
     tail = jnp.exp(last - cum) * rate
-    start = start_ref[...]
-    grad = grad_ref[...]
+    start = both_ref[:, 0].reshape(BLOCK * HEAD_DIM, STATE)
+    grad = both_ref[:, 1].reshape(BLOCK * HEAD_DIM, STATE)
     inner = jnp.sum(fold(start * grad, BLOCK), axis=1, keepdims=True)
     start_low = start.astype(BF16)
     grad_low = grad.astype(BF16)
@@ -169,7 +174,7 @@
         "group": pl.BlockSpec((t, STATE), lambda i: (0, i // per)),
         "one": pl.BlockSpec((BLOCK, 1), lambda i: (i, 0)),
         "flat": flat,
-        "state": pl.BlockSpec((BLOCK * HEAD_DIM, STATE), lambda i: (i, 0)),
+        "state": pl.BlockSpec((BLOCK, 2, HEAD_DIM, STATE), lambda i: (i, 0, 0, 0)),
         "lane": pl.BlockSpec((BLOCK, STATE), lambda i: (i, 0)),
         "groupt": pl.BlockSpec((STATE, t), lambda i: (i // per, 0)),
     }
@@ -190,10 +195,9 @@
         first_kernel,
         grid=(heads // BLOCK,),
         in_specs=[s["nat"], s["nat"], s["rows"], s["group"], s["group"], s["one"], s["one"]],
-        out_specs=[s["state"], s["state"], s["lane"], s["flat"], s["flat"]],
+        out_specs=[s["state"], s["lane"], s["flat"], s["flat"]],
         out_shape=[
-            sds((heads * HEAD_DIM, STATE)),
-            sds((heads * HEAD_DIM, STATE)),
+            sds((heads, 2, HEAD_DIM, STATE)),
             sds((heads, STATE)),
             sds((heads * HEAD_DIM, t), BF16),
             sds((heads * HEAD_DIM, t), BF16),
@@ -226,14 +230,14 @@
     )(dy, raw, b, c, alog, bias, skip, xt, dyt)
 
 
-def final_grads(raw, b, c, alog, bias, xt, dyt, start, grad, inner, per):
+def final_grads(raw, b, c, alog, bias, xt, dyt, both, inner, per):
     heads, t = raw.shape
     s = specs(per, t)
     groups = heads // BLOCK // per
     return pl.pallas_call(
         functools.partial(last_kernel, per),
         grid=(heads // BLOCK,),
-        in_specs=[s["rows"], s["group"], s["group"], s["one"], s["one"], s["flat"], s["flat"], s["state"], s["state"], s["flat"], s["rows"], s["rows"], s["groupt"], s["groupt"]],
+        in_specs=[s["rows"], s["group"], s["group"], s["one"], s["one"], s["flat"], s["flat"], s["state"], s["flat"], s["rows"], s["rows"], s["groupt"], s["groupt"]],
         out_specs=[s["nat"], s["rows"], s["group"], s["group"]],
         out_shape=[
             sds((t, heads * HEAD_DIM), BF16),
@@ -244,55 +248,325 @@
         scratch_shapes=[pltpu.VMEM((STATE, t), F32), pltpu.VMEM((STATE, t), F32)],
         compiler_params=params(32),
         name="final_grads",
-    )(raw, b, c, alog, bias, xt, dyt, start, grad, *inner)
-
-
-def forward_tree(own_end, carries, link_up):
-    node_count = own_end.shape[0]
-    start_state = jnp.zeros_like(own_end)
-    for depth_step in range(TREE_DEPTH - 1):
-        finish = carries * start_state + own_end
-        start_state = jnp.dot(link_up, finish.reshape(node_count, -1), precision=highest).reshape(own_end.shape)
-    return start_state
-
-
-def backward_tree(own_pull, carries, link_down):
-    node_count = own_pull.shape[0]
-    end_grad = jnp.zeros_like(own_pull)
-    for depth_step in range(TREE_DEPTH - 1):
-        start_grad = own_pull + carries * end_grad
-        end_grad = jnp.dot(link_down, start_grad.reshape(node_count, -1), precision=highest).reshape(own_pull.shape)
-    return end_grad
-
-
-def exchange(payload):
-    return lax.all_to_all(payload, "leaf", split_axis=0, concat_axis=0, tiled=True)
+    )(raw, b, c, alog, bias, xt, dyt, both, *inner)
+
+
+def arms(near, pick):
+    def furthest(v):
+        return jnp.max(jnp.where(near, v, 0), axis=1, keepdims=True)
+
+    up = furthest(jnp.where(pick < ARM, pick, 0))
+    down = furthest(jnp.where(pick > ARM, NZ - pick, 0))
+    both = furthest(jnp.where(pick == ARM, 1, 0)) > 0
+    return jnp.where(both & (up >= down), ARM, up), jnp.where(both & (up < down), ARM, down)
+
+
+def tree_kernel(slots, parent_ref, carry_ref, own_ref, both_ref, xin, extra, got, put, res, crow, carried, scale, relay, local, remote, here,
+                own_sem, in_send, in_recv, z_send, z_recv, out_send, out_recv, out_own, carry_send, carry_recv):
+    nodes = NX * NZ
+    part = own_ref.shape[0] // NX
+    half = HEAD_DIM // 2
+    chunks = part * 2
+    rounds = chunks + LAG * (ARM - 1)
+    ahead = 3
+    me = lax.axis_index("leaf")
+    x, z = me // NZ, lax.rem(me, NZ)
+
+    def peer(k):
+        return lax.rem(x + k, NX)
+
+    def at(px, pz):
+        return {"leaf": px * NZ + pz}
+
+    barrier = pltpu.get_barrier_semaphore()
+
+    @pl.loop(1, nodes)
+    def _(k):
+        pl.semaphore_signal(barrier, inc=1, device_id={"leaf": lax.rem(me + k, nodes)}, device_id_type=MESH)
+
+    crow[...] = jnp.zeros_like(crow)
+    crow[0, :, : carry_ref.shape[0]] = carry_ref[...].T[0:1, :]
+    got[:, 0:LAG] = jnp.zeros((2, LAG) + got.shape[2:], F32)
+    pl.semaphore_wait(barrier, nodes - 1)
+
+    def in_copy(hd, k):
+        return pltpu.make_async_remote_copy(
+            src_ref=own_ref.at[peer(k) * part + hd],
+            dst_ref=xin.at[x, hd],
+            send_sem=in_send.at[hd, k - 1],
+            recv_sem=in_recv.at[hd, k - 1],
+            device_id=at(peer(k), z),
+            device_id_type=MESH,
+        )
+
+    def start_in(hd):
+        for k in range(1, NX):
+            in_copy(hd, k).start()
+
+    own_copy = pltpu.make_async_copy(own_ref.at[pl.ds(x * part, part)], xin.at[x], own_sem)
+    own_copy.start()
+    start_in(0)
+
+    def carry_copy(k):
+        return pltpu.make_async_remote_copy(
+            src_ref=crow.at[0],
+            dst_ref=carried.at[me],
+            send_sem=carry_send,
+            recv_sem=carry_recv,
+            device_id={"leaf": lax.rem(me + k, nodes)},
+            device_id_type=MESH,
+        )
+
+    @pl.loop(1, nodes)
+    def _(k):
+        carry_copy(k).start()
+
+    for hd in range(1, ahead):
+        start_in(hd)
+
+    lanes = 128
+    sub = lax.broadcasted_iota(jnp.int32, (nodes, lanes), 0)
+    lane = lax.broadcasted_iota(jnp.int32, (nodes, lanes), 1)
+    par_col = jnp.full((nodes, lanes), -1, jnp.int32)
+    par_row = jnp.full((nodes, lanes), -2, jnp.int32)
+    for n in range(nodes):
+        par_col = jnp.where(sub == n, parent_ref[n], par_col)
+        par_row = jnp.where(lane == n, parent_ref[n], par_row)
+    is_root = par_col < 0
+    near = (par_row == sub) | (is_root & (lane < nodes))
+    up, down = arms(near, (lane - sub) & (NZ - 1))
+    up = jnp.broadcast_to(up, (nodes, lanes))
+    down = jnp.broadcast_to(down, (nodes, lanes))
+
+    def one(v):
+        return jnp.where(v, 1.0, 0.0)
+
+    order = one(lax.broadcasted_iota(jnp.int32, (nodes, nodes), 0) > lax.broadcasted_iota(jnp.int32, (nodes, nodes), 1))
+
+    def edge(e):
+        rising = ((e - sub) & (NZ - 1)) < up
+        falling = ((sub - 1 - e) & (NZ - 1)) < down
+        used = one(rising | falling)
+        rank = dot(order, used)
+        slot = lax.broadcasted_iota(jnp.int32, (slots, nodes, lanes), 0).astype(F32)
+        place = jnp.where(jnp.abs(slot - rank[None]) < 0.5, used[None], 0.0)
+        return one(rising), one(falling), place
+
+    up_in, down_in, place_in = edge(z + NZ - 1)
+    up_out, down_out, place_out = edge(z)
+
+    def total(v):
+        return jnp.sum(v, axis=1, keepdims=True)
+
+    same = up_in * up_out + down_in * down_out
+    for j in range(slots):
+        relay[0, j] = total(place_out * (place_in[j] * same)[None])
+        relay[1, j] = total(place_in * (place_out[j] * same)[None])
+    wants = [one(sub == parent_ref[k * NZ + z]) for k in range(NX)] + [one(is_root)]
+    for k in range(NX):
+        mine = one(sub == k * NZ + z)
+        local[0, k] = total(place_out * (up_out * mine)[None])
+        local[1, k] = total(place_in * (down_in * mine)[None])
+        for m in range(NX + 1):
+            here[k, m] = jnp.sum(wants[m] * mine, axis=0, keepdims=True)
+    for d in range(ARM):
+        far_up = one(((z - sub) & (NZ - 1)) == d + 1) * up_in
+        far_down = one(((sub - z) & (NZ - 1)) == d + 1) * down_out
+        for m in range(NX + 1):
+            remote[0, d, m] = total(place_in * (far_up * wants[m])[None])
+            remote[1, d, m] = total(place_out * (far_down * wants[m])[None])
+
+    for kind in ("send", "recv"):
+        rows = carried.at[0 : nodes - 1]
+        wait = pltpu.make_async_copy(rows, rows, carry_send if kind == "send" else carry_recv)
+        wait.wait()
+    carried[me] = crow[0]
+    decays = carried[:, 0, :]
+    for k in range(NX):
+        row = jnp.sum(jnp.where(is_root, 0.0, wants[k] * decays), axis=0, keepdims=True)
+        scale[k] = jnp.broadcast_to(row, (lanes, lanes)).T[: scale.shape[1], None, :]
+    own_copy.wait()
+
+    def z_copy(way, r):
+        to = lax.rem(z + (1 if way == 0 else NZ - 1), NZ)
+        return pltpu.make_async_remote_copy(
+            src_ref=put.at[way, lax.rem(r, 3)],
+            dst_ref=got.at[way, r + LAG],
+            send_sem=z_send.at[way, lax.rem(r, 3)],
+            recv_sem=z_recv.at[way, r],
+            device_id=at(x, to),
+            device_id_type=MESH,
+        )
+
+    def out_copy(hd, k):
+        return pltpu.make_async_remote_copy(
+            src_ref=res.at[peer(k), hd],
+            dst_ref=both_ref.at[x * part + hd],
+            send_sem=out_send.at[hd, k - 1],
+            recv_sem=out_recv.at[hd, k - 1],
+            device_id=at(peer(k), z),
+            device_id_type=MESH,
+        )
+
+    def own_out(hd):
+        return pltpu.make_async_copy(res.at[x, hd], both_ref.at[x * part + hd], out_own.at[hd])
+
+    def piece(k, chunk, kind):
+        rows = pl.ds(pl.multiple_of(lax.rem(chunk, 2) * half, half), half)
+        return xin[k, chunk // 2, kind, rows, :]
+
+    last = LAG * ARM
+
+    @pl.loop(0, chunks + last)
+    def _(r):
+        @pl.when((r >= LAG) & (r < rounds + LAG))
+        def _():
+            for way in range(2):
+                z_copy(way, r - LAG).wait_recv()
+
+        @pl.when((lax.rem(r, 2) == 0) & (r < chunks))
+        def _():
+            hd = r // 2
+
+            @pl.when(hd + ahead < part)
+            def _():
+                start_in(hd + ahead)
+
+            for k in range(1, NX):
+                in_copy(hd, k).wait_recv()
+            summed = scale[0, x * part + hd] * xin[0, hd, 1]
+            for k in range(1, NX):
+                summed += scale[k, x * part + hd] * xin[k, hd, 1]
+            extra[hd] = summed
+
+        @pl.when(r < rounds)
+        def _():
+            @pl.when(r >= 3)
+            def _():
+                for way in range(2):
+                    z_copy(way, r - 3).wait_send()
+
+            for way in range(2):
+                now = jnp.minimum(r, chunks - 1)
+                acc = local[way, 0] * piece(0, now, 0)[None]
+                for k in range(1, NX):
+                    acc += local[way, k] * piece(k, now, 0)[None]
+                for d in range(ARM):
+                    chunk = jnp.clip(r - LAG * (ARM - 1 - d), 0, chunks - 1)
+                    for k in range(NX):
+                        acc += remote[1 - way, d, k] * piece(k, chunk, 1)[None]
+                    rows = pl.ds(pl.multiple_of(lax.rem(chunk, 2) * half, half), half)
+                    acc += remote[1 - way, d, NX] * extra[chunk // 2, rows, :][None]
+                for j in range(slots):
+                    acc += relay[way, j] * got[way, r, j][None]
+                put[way, lax.rem(r, 3)] = acc
+                z_copy(way, r).start()
+
+        @pl.when(r >= last)
+        def _():
+            c = r - last
+            hd = c // 2
+            rows = pl.ds(pl.multiple_of(lax.rem(c, 2) * half, half), half)
+            begin = here[0] * piece(0, c, 0)[None]
+            for k in range(1, NX):
+                begin += here[k] * piece(k, c, 0)[None]
+            for way in range(2):
+                for d in range(ARM):
+                    for j in range(slots):
+                        begin += remote[way, d, :, j] * got[way, c + LAG * (d + 1), j][None]
+            end = here[:, NX] * extra[hd, rows, :][None]
+            for k in range(NX):
+                end += here[:, k] * piece(k, c, 1)[None]
+            for way in range(2):
+                for j in range(slots):
+                    end += local[1 - way, :, j] * got[way, c + LAG * ARM, j][None]
+            for k in range(NX):
+                res[k, hd, 0, rows, :] = begin[k] + scale[k, x * part + hd] * begin[NX]
+                res[k, hd, 1, rows, :] = end[k]
+
+            @pl.when(lax.rem(c, 2) == 1)
+            def _():
+                for k in range(1, NX):
+                    out_copy(hd, k).start()
+                own_out(hd).start()
+
+    for way in range(2):
+        for r in range(rounds - 3, rounds):
+            z_copy(way, r).wait_send()
+
+    @pl.loop(0, part)
+    def _(hd):
+        for k in range(1, NX):
+            in_copy(hd, k).wait_send()
+            out_copy(hd, k).wait()
+        own_out(hd).wait()
+
+
+def tree(slots, parent, carry, own):
+    heads = own.shape[0]
+    part = heads // NX
+    half = HEAD_DIM // 2
+    rounds = part * 2 + LAG * (ARM - 1)
+    dma = pltpu.SemaphoreType.DMA
+    return pl.pallas_call(
+        functools.partial(tree_kernel, slots),
+        in_specs=[pl.BlockSpec(memory_space=pltpu.SMEM), pl.BlockSpec(memory_space=pltpu.VMEM), pl.BlockSpec(memory_space=pl.ANY)],
+        out_specs=pl.BlockSpec(memory_space=pl.ANY),
+        out_shape=sds(own.shape),
+        scratch_shapes=[
+            pltpu.VMEM((NX, part, 2, HEAD_DIM, STATE), F32),
+            pltpu.VMEM((part, HEAD_DIM, STATE), F32),
+            pltpu.VMEM((2, rounds + LAG, slots, half, STATE), F32),
+            pltpu.VMEM((2, 3, slots, half, STATE), F32),
+            pltpu.VMEM((NX, part, 2, HEAD_DIM, STATE), F32),
+            pltpu.VMEM((1, 1, STATE), F32),
+            pltpu.VMEM((NX * NZ, 1, STATE), F32),
+            pltpu.VMEM((NX, heads, 1, STATE), F32),
+            pltpu.VMEM((2, slots, slots, 1, STATE), F32),
+            pltpu.VMEM((2, NX, slots, 1, STATE), F32),
+            pltpu.VMEM((2, ARM, NX + 1, slots, 1, STATE), F32),
+            pltpu.VMEM((NX, NX + 1, 1, STATE), F32),
+            dma,
+            dma((part, NX - 1)),
+            dma((part, NX - 1)),
+            dma((2, 3)),
+            dma((2, rounds)),
+            dma((part, NX - 1)),
+            dma((part, NX - 1)),
+            dma((part,)),
+            dma,
+            dma,
+        ],
+        compiler_params=pltpu.CompilerParams(collective_id=slots, has_side_effects=True, vmem_limit_bytes=56 << 20),
+        name=f"tree_{slots}",
+    )(parent, carry, own)
+
+
+FEW = 7
+ALL = 13
+
+
+def busiest(parent):
+    nodes = NX * NZ
+    i = jnp.arange(nodes, dtype=jnp.int32)
+    near = (parent[None, :] == i[:, None]) | (parent < 0)[:, None]
+    up, down = arms(near, (i[None, :] - i[:, None]) & (NZ - 1))
+    e = jnp.arange(NZ, dtype=jnp.int32)[None, :]
+    used = (((e - i[:, None]) & (NZ - 1)) < up) | (((i[:, None] - 1 - e) & (NZ - 1)) < down)
+    return jnp.max(jnp.sum(used.astype(jnp.int32), axis=0))
 
 
 def body(inputs, dt_raw, b_proj, c_proj, a_log, dt_bias, skip, grad_out, parent, children):
     heads = a_log.shape[0]
     groups = b_proj.shape[2] // STATE
     per = heads // BLOCK // groups
-    nodes = parent.shape[0]
     x, dy, raw, b, c = inputs[0], grad_out[0], dt_raw[0], b_proj[0], c_proj[0]
     alog, bias, skips = a_log[:, None], dt_bias[:, None], skip[:, None]
-    own_end, own_pull, carry, xt, dyt = summaries(x, dy, raw, b, c, alog, bias, per)
-    node_ids = jnp.arange(nodes, dtype=jnp.int32)
-    link_up = (parent[:, None] == node_ids[None, :]).astype(F32)
-    link_down = jnp.any(children[:, :, None] == node_ids[None, None, :], axis=1).astype(F32)
-
-    share = heads // nodes
-
-    def as_slices(flat):
-        return flat.reshape(nodes, share * HEAD_DIM, STATE)
-
-    carry_slices = jnp.repeat(exchange(carry).reshape(nodes, share, STATE), HEAD_DIM, axis=1)
-    start_slices = forward_tree(as_slices(exchange(own_end)), carry_slices, link_up)
-    start = exchange(start_slices.reshape(heads * HEAD_DIM, STATE))
+    few = lax.pmax(busiest(parent), "dp") <= FEW
+    own, carry, xt, dyt = summaries(x, dy, raw, b, c, alog, bias, per)
     inner = inner_grads(dy, raw, b, c, alog, bias, skips, xt, dyt, per)
-    grad_slices = backward_tree(as_slices(exchange(own_pull)), carry_slices, link_down)
-    grad = exchange(grad_slices.reshape(heads * HEAD_DIM, STATE))
-    gx, gdt, gb, gc = final_grads(raw, b, c, alog, bias, xt, dyt, start, grad, inner, per)
+    both = lax.cond(few, functools.partial(tree, FEW), functools.partial(tree, ALL), parent, carry, own)
+    gx, gdt, gb, gc = final_grads(raw, b, c, alog, bias, xt, dyt, both, inner, per)
     return gx[None], gdt[None], gb[None], gc[None]
 
 

time: 283 us -> 188 us (0.66)
  Pallas kernels: 32.8 us -> 163 us
  waiting for transfers between devices: 116 us -> 0 us
  blocking collectives: 74.1 us -> 8.56 us
  starting transfers between devices: 17.2 us -> 0 us
  local copies, waits for them, and re-layouts: 24.7 us -> 13.3 us
  matrix products: 9.35 us -> 0 us
  other arithmetic: 7.38 us -> 0.99 us
    pallas_call x0 -> x1, Pallas kernels: none -> 131 us  [tree(): pl.pallas_call(functools.partial(tree_kernel, slots), in_specs=[pl.BlockS...]
    all_to_all x3 -> x0, waiting for transfers between devices: 116 us -> none  [exchange(): lax.all_to_all(payload, 'leaf', split_axis=0, concat_axis=0, tiled=True)]
    all_to_all x2 -> x0, blocking collectives: 74.1 us -> none  [exchange(): lax.all_to_all(payload, 'leaf', split_axis=0, concat_axis=0, tiled=True)]
    all_to_all x3 -> x0, starting transfers between devices: 17.2 us -> none  [exchange(): lax.all_to_all(payload, 'leaf', split_axis=0, concat_axis=0, tiled=True)]
    dot_general x4 -> x0, matrix products: 9.35 us -> none  [the longest x2 5.77 us: backward_tree(): jnp.dot(link_down, start_grad.reshape(node_count, -1), precision=highest)]
    pmax x0 -> x1, blocking collectives: none -> 8.56 us  [body(): few = lax.pmax(busiest(parent), 'dp') <= FEW]
    unnamed x1 -> x0, other arithmetic: 7.24 us -> none
    unnamed x40 -> x34, local copies, waits for them, and re-layouts: 17.9 us -> 11.7 us
  transfers between devices with their start and end apart: 3 -> 0, of which waited for: 3 -> 0; matrix products, arithmetic and copies ran while one was open for 3% -> 0% of each run, Pallas kernels for 6% -> 0%
where the time goes in v2:
time: 188 us; the launch traced here: 187 us
  Pallas kernels  163 us (87%)
  local copies, waits for them, and re-layouts  13.3 us (7%)
  blocking collectives  8.56 us (5%)
    pallas_call x1, Pallas kernels, tree(): pl.pallas_call(functools.partial(tree_kernel, slots), in_specs=[pl.BlockS...  131 us
    pallas_call x1, Pallas kernels, inner_grads(): pl.pallas_call(functools.partial(inner_kernel, per), grid=(heads // BLOCK...  16.9 us
    unnamed x34, local copies, waits for them, and re-layouts  11.7 us
    pmax x1, blocking collectives, body(): few = lax.pmax(busiest(parent), 'dp') <= FEW  8.56 us
    pallas_call x1, Pallas kernels, final_grads(): pl.pallas_call(functools.partial(last_kernel, per), grid=(heads // BLOCK,...  7.63 us
    pallas_call x1, Pallas kernels, summaries(): pl.pallas_call(first_kernel, grid=(heads // BLOCK,), in_specs=[s['nat'],...  6.85 us

profile of v2, /device:TPU:16, one launch (start us, length us, event | category | flops | bytes accessed | tf_op | source)
XLA Modules:
  0.0 187.3 jit_solution(7338466919073491632)
XLA Ops:
  0.6 0.0 copy-start.15
  0.6 0.8 copy.25.alog_ref
  1.4 0.7 copy.26.bias_ref
  2.1 0.0 copy-start
  2.1 1.6 copy-done
  3.7 0.0 copy-start.1
  3.7 1.6 copy-done.1
  5.3 0.0 copy-start.8
  5.3 0.9 copy-done.8
  6.2 0.0 copy-start.10
  6.2 0.9 copy-done.10
  7.1 0.0 copy-start.12
  7.1 0.8 copy-done.12
  8.0 6.9 %summaries.1 = (f32[64,2,64,128]{3,2,1,0:T(8,128)}, f32[64,128]{1,0:T(8,128)S(1)}, bf16[4096,256]{1,0:T(8,128)(2,1)S(1)}, bf16[4096,256]{1,0:T(8,128)(2,1)S(1)}) custom-call(bf16[256,4096]{1,0:T(8,128)(2,1)S(1)} %bitcast.12, bf16[256,4096]{1,0:T(8,128)(2,1)S(1)} %bitcast.13, f32[64,256]{1,0:T(8,128)S(1)} %bitcast.21, bf16[256,256]{1,0:T(8,128)(2,1)S(1)} %bitcast.15, ...), custom_call_target="tpu_custom_call" | custom-call | tf_op jit(solution)/shard_map/summaries/pallas_call | solution.py:194
  14.8 0.0 copy-start.3
  14.8 1.3 copy-done.3
  16.1 0.0 copy-start.6
  16.1 1.4 copy-done.6
  17.5 0.0 copy-done.15
  17.5 0.2 select_reduce_fusion.1
  17.7 0.1 convert_reduce_fusion
  17.9 0.6 reduce_max.39
  18.5 8.6 %pmax.7 = s32[]{:T(128)} all-reduce(s32[]{:T(128)} %reduce_max.39), channel_id=1, replica_groups=mesh['leaf'=32,'heads'=2,'dp'=4] {'dp'}, use_global_device_ids=true, to_apply=%region_5.6 | all-reduce | flops 1 | bytes 8 | tf_op jit(solution)/shard_map/pmax | solution.py:565
  27.7 0.0 copy-start.16
  27.7 0.0 copy-start.2
  27.7 0.0 copy-start.9
  27.7 0.0 copy-start.11
  27.8 0.0 copy-start.13
  27.8 131.6 %conditional.1 = (f32[64,2,64,128]{3,2,1,0:T(8,128)}) conditional(s32[]{:T(128)} %convert_element_type.7, (s32[32]{0:T(128)S(1)}, f32[64,128]{1,0:T(8,128)S(1)}, f32[64,2,64,128]{3,2,1,0:T(8,128)}) %tuple.22, (s32[32]{0:T(128)S(1)}, f32[64,128]{1,0:T(8,128)S(1)}, f32[64,2,64,128]{3,2,1,0:T(8,128)}) %tuple.23), branch_computations={%region_6.7_spmd, %region_7.8_spmd} | conditional | bytes 8 | solution.py:568
  27.8 131.4 %tree_7.1 = f32[64,2,64,128]{3,2,1,0:T(8,128)} custom-call(s32[32]{0:T(128)S(1)} %get-tuple-element.18.parent_ref, f32[64,128]{1,0:T(8,128)S(1)} %get-tuple-element.19.carry_ref, f32[64,2,64,128]{3,2,1,0:T(8,128)} %get-tuple-element.20.own_ref), custom_call_target="tpu_custom_call" | custom-call | tf_op jit(solution)/shard_map/cond/branch_1_fun/tree_7/pallas_call | solution.py:511
  159.3 0.0 copy-done.16
  159.3 0.1 copy.24.skip_ref
  159.4 0.0 copy-done.2
  159.4 0.0 copy-done.9
  159.5 0.0 copy-done.11
  159.5 0.0 copy-done.13
  159.5 0.0 copy-start.4
  159.5 1.6 copy-done.4
  161.1 0.0 copy-start.7
  161.1 1.6 copy-done.7
  162.7 0.0 copy-start.5
  162.7 0.0 copy-start.14
  162.7 16.9 %inner_grads.1 = (f32[4096,256]{1,0:T(8,128)S(1)}, f32[64,256]{1,0:T(8,128)S(1)}, f32[64,256]{1,0:T(8,128)S(1)}, f32[256,256]{1,0:T(8,128)S(1)}, f32[256,256]{1,0:T(8,128)S(1)}) custom-call(bf16[256,4096]{1,0:T(8,128)(2,1)S(1)} %bitcast.14, f32[64,256]{1,0:T(8,128)S(1)} %bitcast.22, bf16[256,256]{1,0:T(8,128)(2,1)S(1)} %bitcast.16, ...), custom_call_target="tpu_custom_call" | custom-call | flops 1073741824 | bytes 8388608 | tf_op jit(solution)/shard_map/inner_grads/pallas_call | solution.py:214
  179.6 0.0 copy-done.5
  179.6 0.0 copy-done.14
  179.6 7.6 %final_grads.1 = (bf16[256,4096]{1,0:T(8,128)(2,1)}, f32[64,256]{1,0:T(8,128)}, f32[256,256]{1,0:T(8,128)}, f32[256,256]{1,0:T(8,128)}) custom-call(f32[64,256]{1,0:T(8,128)S(1)} %bitcast.23, bf16[256,256]{1,0:T(8,128)(2,1)S(1)} %bitcast.17, bf16[256,256]{1,0:T(8,128)(2,1)S(1)} %bitcast.20, f32[64,1]{1,0:T(8,128)S(1)} %copy.25.alog_ref, ...), custom_call_target="tpu_custom_call" | custom-call | tf_op jit(solution)/shard_map/final_grads/pallas_call | solution.py:237
  (2 shorter events, 0.0 us)
Async XLA Ops:
  0.6 16.9 %copy-start.15 = (s32[32]{0:T(128)S(1)}, s32[32]{0:T(128)}, u32[]{:S(2)}) copy-start(s32[32]{0:T(128)} %param.20) | copy-start | bytes 388
  2.1 1.6 copy-start
  3.7 1.6 copy-start.1
  5.3 0.9 copy-start.8
  6.2 0.9 copy-start.10
  7.1 0.8 copy-start.12
  14.8 1.3 copy-start.3
  16.1 1.4 copy-start.6
  27.7 131.6 %copy-start.16 = (f32[64]{0:T(128)S(1)}, f32[64]{0:T(128)}, u32[]{:S(2)}) copy-start(f32[64]{0:T(128)} %param.18) | copy-start | bytes 772
  27.7 131.7 %copy-start.2 = (bf16[1,256,4096]{2,1,0:T(8,128)(2,1)S(1)}, bf16[1,256,4096]{2,1,0:T(8,128)(2,1)}, u32[]{:S(2)}) copy-start(bf16[1,256,4096]{2,1,0:T(8,128)(2,1)} %param.19) | copy-start | bytes 6291460
  27.7 131.7 %copy-start.9 = (bf16[1,256,256]{2,1,0:T(8,128)(2,1)S(1)}, bf16[1,256,256]{2,1,0:T(8,128)(2,1)}, u32[]{:S(2)}) copy-start(bf16[1,256,256]{2,1,0:T(8,128)(2,1)} %param.14) | copy-start | bytes 393220
  27.7 131.7 %copy-start.11 = (bf16[1,256,256]{2,1,0:T(8,128)(2,1)S(1)}, bf16[1,256,256]{2,1,0:T(8,128)(2,1)}, u32[]{:S(2)}) copy-start(bf16[1,256,256]{2,1,0:T(8,128)(2,1)} %param.15) | copy-start | bytes 393220
  27.8 131.7 %copy-start.13 = (f32[1,64,256]{2,1,0:T(8,128)S(1)}, f32[1,64,256]{2,1,0:T(8,128)}, u32[]{:S(2)}) copy-start(f32[1,64,256]{2,1,0:T(8,128)} %param.13) | copy-start | bytes 196612
  159.5 1.6 copy-start.4
  161.1 1.6 copy-start.7
  162.7 17.0 %copy-start.5 = (bf16[4096,256]{1,0:T(8,128)(2,1)S(1)}, bf16[4096,256]{1,0:T(8,128)(2,1)}, u32[]{:S(2)}) copy-start(bf16[4096,256]{1,0:T(8,128)(2,1)} %copy-done.3) | copy-start | bytes 6291460
  162.7 17.0 %copy-start.14 = (f32[64,2,64,128]{3,2,1,0:T(8,128)S(1)}, f32[64,2,64,128]{3,2,1,0:T(8,128)}, u32[]{:S(2)}) copy-start(f32[64,2,64,128]{3,2,1,0:T(8,128)} %get-tuple-element.57.both_ref) | copy-start | bytes 12582916

commit v3 on v2

--- a/solution.py
+++ b/solution.py
@@ -13,7 +13,7 @@
 NX = 4
 NZ = 8
 ARM = 4
-LAG = 2
+LAG = 3
 F32 = jnp.float32
 BF16 = jnp.bfloat16
 
@@ -54,7 +54,7 @@
     return flat.reshape(heads, -1, flat.shape[1]).sum(axis=1)
 
 
-def first_kernel(x_ref, dy_ref, raw_ref, b_ref, c_ref, alog_ref, bias_ref, own_ref, carry_ref, xt_ref, dyt_ref):
+def first_kernel(x_ref, dy_ref, raw_ref, b_ref, c_ref, alog_ref, bias_ref, own_ref, carry_ref, xt_ref, dyt_ref, rise_ref, fall_ref):
     rate, cum = rates(raw_ref[...], alog_ref[...], bias_ref[...])
     last = cum[:, -1:]
     tail = jnp.exp(last - cum) * rate
@@ -68,61 +68,71 @@
     own_ref[:, 0] = end.reshape(BLOCK, HEAD_DIM, STATE)
     own_ref[:, 1] = pull.reshape(BLOCK, HEAD_DIM, STATE)
     carry_ref[...] = jnp.broadcast_to(jnp.exp(last), carry_ref.shape)
-
-
-def inner_kernel(per, dy_ref, raw_ref, b_ref, c_ref, alog_ref, bias_ref, skip_ref, xt_ref, dyt_ref, dx_ref, row_ref, col_ref, dbt_ref, dct_ref, score, total):
-    t = raw_ref.shape[1]
+    rise = cum.T
+    fall = jnp.log(rate) - cum
+    for i in range(BLOCK // 2):
+        rise_ref[i] = rise[:, 2 * i : 2 * i + 2]
+        fall_ref[i] = fall[2 * i : 2 * i + 2]
+
+
+def inner_pair(pair, per, skip_ref, dy_ref, b_ref, c_ref, xt_ref, dyt_ref, rise_ref, fall_ref, dx_ref, row_ref, col_ref, dbt_ref, dct_ref, score, summed):
+    t = dy_ref.shape[0]
     half = t // 2
-    step = pl.program_id(0)
-
-    @pl.when(step % per == 0)
+    both = 2 * HEAD_DIM
+    group = pl.ds(pl.multiple_of(pair // per * STATE, STATE), STATE)
+
+    @pl.when(lax.rem(pair, per) == 0)
     def _():
-        score[...] = dot(c_ref[...], b_ref[...], 1, 1)
-        total[...] = jnp.zeros_like(total)
-
-    rate, cum = rates(raw_ref[...], alog_ref[...], bias_ref[...])
-    rowterm = jnp.log(rate) - cum
-    cumt = cum.T
-    r = lax.broadcasted_iota(jnp.int32, (half, half), 0)
-    c = lax.broadcasted_iota(jnp.int32, (half, half), 1)
-    causal = r >= c
-    lane = lax.broadcasted_iota(jnp.int32, (2 * HEAD_DIM, t), 0)
-    lefts = []
-    for i in range(BLOCK):
-        pair = slice(i // 2 * 2 * HEAD_DIM, (i // 2 + 1) * 2 * HEAD_DIM)
-        mine = slice(i * HEAD_DIM, (i + 1) * HEAD_DIM)
-        xpair = xt_ref[pair, :]
-        xhead = jnp.where((lane // HEAD_DIM) == i % 2, xpair, jnp.zeros_like(xpair))
-        dyh = dyt_ref[mine, :]
-        skip = skip_ref[i:i + 1, :]
+        score[...] = dot(c_ref[:, group], b_ref[:, group], 1, 1)
+        summed[...] = jnp.zeros_like(summed)
+
+    mine = pl.ds(pl.multiple_of(pair * both, both), both)
+    rise = rise_ref[pair]
+    fall = fall_ref[pair]
+    xpair = xt_ref[mine, :]
+    dypair = dyt_ref[mine, :]
+    dycols = dy_ref[:, mine]
+    causal = lax.broadcasted_iota(jnp.int32, (half, half), 0) >= lax.broadcasted_iota(jnp.int32, (half, half), 1)
+    where_x = lax.broadcasted_iota(jnp.int32, (both, t), 0) // HEAD_DIM
+    lefts, downs, outs = [], [], []
+    for i in range(2):
+        xhead = jnp.where(where_x == i, xpair, jnp.zeros_like(xpair))
+        dyh = dypair[i * HEAD_DIM : (i + 1) * HEAD_DIM]
+        skip = skip_ref[2 * pair + i]
         parts = {}
         for a, b in ((0, 0), (1, 0), (1, 1)):
             rows = slice(a * half, (a + 1) * half)
             cols = slice(b * half, (b + 1) * half)
-            gap = cumt[rows, i:i + 1] + rowterm[i:i + 1, cols]
+            gap = rise[rows, i : i + 1] + fall[i : i + 1, cols]
             if a == b:
                 gap = jnp.where(causal, gap, -1e30)
             decay = jnp.exp(gap)
             mix = decay * score[rows, cols]
-            dmix = dot(dy_ref[rows, pair], xhead[:, cols])
-            total[rows, cols] += dmix * decay
+            dmix = dot(dycols[rows], xhead[:, cols])
+            summed[rows, cols] += dmix * decay
             parts[a, b] = (mix.astype(BF16), dmix * mix)
         q0, q1, q2 = parts[0, 0][1], parts[1, 0][1], parts[1, 1][1]
-        col_ref[i:i + 1, :half] = jnp.sum(q0 + q1, axis=0, keepdims=True)
-        col_ref[i:i + 1, half:] = jnp.sum(q2, axis=0, keepdims=True)
-        lefts.append(jnp.concatenate([jnp.sum(q0, axis=1, keepdims=True), jnp.sum(q1 + q2, axis=1, keepdims=True)], axis=0))
+        downs.append(
+            jnp.concatenate([jnp.sum(q0 + q1, axis=0, keepdims=True), jnp.sum(q2, axis=0, keepdims=True)], axis=1)
+        )
+        lefts.append(
+            jnp.concatenate([jnp.sum(q0, axis=1, keepdims=True), jnp.sum(q1 + q2, axis=1, keepdims=True)], axis=0)
+        )
         left = jnp.concatenate([parts[0, 0][0], parts[1, 0][0]], axis=0)
-        dx_ref[mine, :half] = dot(dyh, left) + skip * dyh[:, :half].astype(F32)
-        dx_ref[mine, half:] = dot(dyh[:, half:], parts[1, 1][0]) + skip * dyh[:, half:].astype(F32)
-    row_ref[...] = jnp.concatenate(lefts, axis=1).T
-
-    @pl.when(step % per == per - 1)
+        outs.append(
+            jnp.concatenate([dot(dyh, left), dot(dyh[:, half:], parts[1, 1][0])], axis=1) + skip * dyh.astype(F32)
+        )
+    dx_ref[mine, :] = jnp.concatenate(outs, axis=0)
+    col_ref[pair] = jnp.concatenate(downs, axis=0)
+    row_ref[pair] = jnp.concatenate(lefts, axis=1).T
+
+    @pl.when(lax.rem(pair, per) == per - 1)
     def _():
-        summed = jnp.where(
-            lax.broadcasted_iota(jnp.int32, (t, t), 0) >= lax.broadcasted_iota(jnp.int32, (t, t), 1), total[...], 0.0
-        ).astype(BF16)
-        dbt_ref[...] = dot(c_ref[...], summed, 0, 0)
-        dct_ref[...] = dot(b_ref[...], summed, 0, 1)
+        r = lax.broadcasted_iota(jnp.int32, (t, t), 0)
+        c = lax.broadcasted_iota(jnp.int32, (t, t), 1)
+        low = jnp.where(r >= c, summed[...], 0.0).astype(BF16)
+        dbt_ref[group, :] = dot(c_ref[:, group], low, 0, 0)
+        dct_ref[group, :] = dot(b_ref[:, group], low, 0, 1)
 
 
 def last_kernel(per, raw_ref, b_ref, c_ref, alog_ref, bias_ref, xt_ref, dyt_ref, both_ref, dx_ref, row_ref, col_ref, dbt_ref, dct_ref, gx_ref, gdt_ref, gb_ref, gc_ref, sumb, sumc):
@@ -153,8 +163,9 @@
     carried = dot(start_low, c_ref[...], 1, 1)
     g = fold(dyt.astype(F32) * carried, BLOCK) * growth
     sumc[...] += dot(start_low, spread(growth, dyt).astype(BF16), 0, 0)
-    col = col_ref[...]
-    dcum = row_ref[...] - col + g - z
+    col = jnp.concatenate([col_ref[i] for i in range(BLOCK // 2)], axis=0)
+    row = jnp.concatenate([row_ref[i] for i in range(BLOCK // 2)], axis=0)
+    dcum = row - col + g - z
     at_end = jnp.sum(z, axis=1, keepdims=True) + growth[:, -1:] * inner
     dlog = prefix(dcum, triangle(t, True)) + at_end
     slope = 1.0 / (1.0 + jnp.exp(-v))
@@ -176,6 +187,8 @@
         "flat": flat,
         "state": pl.BlockSpec((BLOCK, 2, HEAD_DIM, STATE), lambda i: (i, 0, 0, 0)),
         "lane": pl.BlockSpec((BLOCK, STATE), lambda i: (i, 0)),
+        "rise": pl.BlockSpec((BLOCK // 2, t, 2), lambda i: (i, 0, 0)),
+        "pairs": pl.BlockSpec((BLOCK // 2, 2, t), lambda i: (i, 0, 0)),
         "groupt": pl.BlockSpec((STATE, t), lambda i: (i // per, 0)),
     }
 
@@ -195,39 +208,18 @@
         first_kernel,
         grid=(heads // BLOCK,),
         in_specs=[s["nat"], s["nat"], s["rows"], s["group"], s["group"], s["one"], s["one"]],
-        out_specs=[s["state"], s["lane"], s["flat"], s["flat"]],
+        out_specs=[s["state"], s["lane"], s["flat"], s["flat"], s["rise"], s["pairs"]],
         out_shape=[
             sds((heads, 2, HEAD_DIM, STATE)),
             sds((heads, STATE)),
             sds((heads * HEAD_DIM, t), BF16),
             sds((heads * HEAD_DIM, t), BF16),
+            sds((heads // 2, t, 2)),
+            sds((heads // 2, 2, t)),
         ],
-        compiler_params=params(32),
+        compiler_params=params(60),
         name="summaries",
     )(x, dy, raw, b, c, alog, bias)
-
-
-def inner_grads(dy, raw, b, c, alog, bias, skip, xt, dyt, per):
-    heads, t = raw.shape
-    s = specs(per, t)
-    groups = heads // BLOCK // per
-    return pl.pallas_call(
-        functools.partial(inner_kernel, per),
-        grid=(heads // BLOCK,),
-        in_specs=[s["nat"], s["rows"], s["group"], s["group"], s["one"], s["one"], s["one"], s["flat"], s["flat"]],
-        out_specs=[s["flat"], s["rows"], s["rows"], s["groupt"], s["groupt"]],
-        out_shape=[
-            sds((heads * HEAD_DIM, t)),
-            sds((heads, t)),
-            sds((heads, t)),
-            sds((groups * STATE, t)),
-            sds((groups * STATE, t)),
-        ],
-        scratch_shapes=[pltpu.VMEM((t, t), F32), pltpu.VMEM((t, t), F32)],
-        compiler_params=params(32),
-        cost_estimate=pl.CostEstimate(flops=heads * t * t * 256, bytes_accessed=heads * t * 512, transcendentals=heads * t * t),
-        name="inner_grads",
-    )(dy, raw, b, c, alog, bias, skip, xt, dyt)
 
 
 def final_grads(raw, b, c, alog, bias, xt, dyt, both, inner, per):
@@ -237,7 +229,7 @@
     return pl.pallas_call(
         functools.partial(last_kernel, per),
         grid=(heads // BLOCK,),
-        in_specs=[s["rows"], s["group"], s["group"], s["one"], s["one"], s["flat"], s["flat"], s["state"], s["flat"], s["rows"], s["rows"], s["groupt"], s["groupt"]],
+        in_specs=[s["rows"], s["group"], s["group"], s["one"], s["one"], s["flat"], s["flat"], s["state"], s["flat"], s["pairs"], s["pairs"], s["groupt"], s["groupt"]],
         out_specs=[s["nat"], s["rows"], s["group"], s["group"]],
         out_shape=[
             sds((t, heads * HEAD_DIM), BF16),
@@ -246,7 +238,7 @@
             sds((t, groups * STATE)),
         ],
         scratch_shapes=[pltpu.VMEM((STATE, t), F32), pltpu.VMEM((STATE, t), F32)],
-        compiler_params=params(32),
+        compiler_params=params(60),
         name="final_grads",
     )(raw, b, c, alog, bias, xt, dyt, both, *inner)
 
@@ -261,7 +253,14 @@
     return jnp.where(both & (up >= down), ARM, up), jnp.where(both & (up < down), ARM, down)
 
 
-def tree_kernel(slots, parent_ref, carry_ref, own_ref, both_ref, xin, extra, got, put, res, crow, carried, scale, relay, local, remote, here,
+def tree_kernel(slots, dps, per, parent_ref, carry_ref, own_ref, *refs):
+    ins, refs = (refs[:8], refs[8:]) if per else ((), refs)
+    (both_ref, most_ref), refs = refs[:2], refs[2:]
+    outs, refs = (refs[:5], refs[5:]) if per else ((), refs)
+    tree_steps(slots, dps, per, parent_ref, carry_ref, own_ref, ins, both_ref, most_ref, outs, refs[25:], *refs[:25])
+
+
+def tree_steps(slots, dps, per, parent_ref, carry_ref, own_ref, ins, both_ref, most_ref, outs, temps, counts, count_send, count_recv, xin, extra, got, put, res, crow, carried, scale, relay, local, remote, here,
                 own_sem, in_send, in_recv, z_send, z_recv, out_send, out_recv, out_own, carry_send, carry_recv):
     nodes = NX * NZ
     part = own_ref.shape[0] // NX
@@ -279,6 +278,9 @@
         return {"leaf": px * NZ + pz}
 
     barrier = pltpu.get_barrier_semaphore()
+    tree_at = lax.axis_index("dp")
+    for k in range(1, dps):
+        pl.semaphore_signal(barrier, inc=1, device_id={"dp": lax.rem(tree_at + k, dps)}, device_id_type=MESH)
 
     @pl.loop(1, nodes)
     def _(k):
@@ -287,7 +289,7 @@
     crow[...] = jnp.zeros_like(crow)
     crow[0, :, : carry_ref.shape[0]] = carry_ref[...].T[0:1, :]
     got[:, 0:LAG] = jnp.zeros((2, LAG) + got.shape[2:], F32)
-    pl.semaphore_wait(barrier, nodes - 1)
+    pl.semaphore_wait(barrier, nodes + dps - 2)
 
     def in_copy(hd, k):
         return pltpu.make_async_remote_copy(
@@ -343,14 +345,38 @@
 
     order = one(lax.broadcasted_iota(jnp.int32, (nodes, nodes), 0) > lax.broadcasted_iota(jnp.int32, (nodes, nodes), 1))
 
+    def users(e):
+        return ((e - sub) & (NZ - 1)) < up, ((sub - 1 - e) & (NZ - 1)) < down
+
+    def used_by(e):
+        rising, falling = users(e)
+        return one(rising | falling)
+
     def edge(e):
-        rising = ((e - sub) & (NZ - 1)) < up
-        falling = ((sub - 1 - e) & (NZ - 1)) < down
-        used = one(rising | falling)
+        rising, falling = users(e)
+        used = used_by(e)
         rank = dot(order, used)
         slot = lax.broadcasted_iota(jnp.int32, (slots, nodes, lanes), 0).astype(F32)
         place = jnp.where(jnp.abs(slot - rank[None]) < 0.5, used[None], 0.0)
         return one(rising), one(falling), place
+
+    busy = jnp.zeros((1, lanes), F32)
+    for e in range(NZ):
+        busy = jnp.maximum(busy, jnp.sum(used_by(e), axis=0, keepdims=True))
+    counts[tree_at] = busy
+
+    def count_copy(k):
+        return pltpu.make_async_remote_copy(
+            src_ref=counts.at[tree_at],
+            dst_ref=counts.at[tree_at],
+            send_sem=count_send.at[k - 1],
+            recv_sem=count_recv.at[k - 1],
+            device_id={"dp": lax.rem(tree_at + k, dps)},
+            device_id_type=MESH,
+        )
+
+    for k in range(1, dps):
+        count_copy(k).start()
 
     up_in, down_in, place_in = edge(z + NZ - 1)
     up_out, down_out, place_out = edge(z)
@@ -490,6 +516,18 @@
                     out_copy(hd, k).start()
                 own_out(hd).start()
 
+        if per:
+
+            @pl.when(r < ins[0].shape[0] // 2)
+            def _():
+                inner_pair(r, per, *ins, *outs, *temps)
+
+    for k in range(1, dps):
+        count_copy(k).wait()
+    most = counts[0]
+    for k in range(1, dps):
+        most = jnp.maximum(most, counts[k])
+    most_ref[...] = jnp.broadcast_to(most, most_ref.shape)
     for way in range(2):
         for r in range(rounds - 3, rounds):
             z_copy(way, r).wait_send()
@@ -502,18 +540,35 @@
         own_out(hd).wait()
 
 
-def tree(slots, parent, carry, own):
+def tree(slots, dps, parent, carry, own, inner=()):
     heads = own.shape[0]
     part = heads // NX
     half = HEAD_DIM // 2
     rounds = part * 2 + LAG * (ARM - 1)
     dma = pltpu.SemaphoreType.DMA
+    vmem = pl.BlockSpec(memory_space=pltpu.VMEM)
+    outs, temps, per = [], [], 0
+    if inner:
+        t, groups = inner[1].shape[0], inner[2].shape[1] // STATE
+        per = heads // 2 // groups
+        outs = [
+            sds((heads * HEAD_DIM, t)),
+            sds((heads // 2, 2, t)),
+            sds((heads // 2, 2, t)),
+            sds((groups * STATE, t)),
+            sds((groups * STATE, t)),
+        ]
+        temps = [pltpu.VMEM((t, t), F32), pltpu.VMEM((t, t), F32)]
     return pl.pallas_call(
-        functools.partial(tree_kernel, slots),
-        in_specs=[pl.BlockSpec(memory_space=pltpu.SMEM), pl.BlockSpec(memory_space=pltpu.VMEM), pl.BlockSpec(memory_space=pl.ANY)],
-        out_specs=pl.BlockSpec(memory_space=pl.ANY),
-        out_shape=sds(own.shape),
+        functools.partial(tree_kernel, slots, dps, per),
+        in_specs=[pl.BlockSpec(memory_space=pltpu.SMEM), vmem, pl.BlockSpec(memory_space=pl.ANY)]
+        + ([pl.BlockSpec(memory_space=pltpu.SMEM)] + [vmem] * 7 if inner else []),
+        out_specs=[pl.BlockSpec(memory_space=pl.ANY), vmem] + [vmem] * len(outs),
+        out_shape=[sds(own.shape), sds((8, STATE))] + outs,
         scratch_shapes=[
+            pltpu.VMEM((dps, 1, STATE), F32),
+            dma((dps,)),
+            dma((dps,)),
             pltpu.VMEM((NX, part, 2, HEAD_DIM, STATE), F32),
             pltpu.VMEM((part, HEAD_DIM, STATE), F32),
             pltpu.VMEM((2, rounds + LAG, slots, half, STATE), F32),
@@ -536,37 +591,35 @@
             dma((part,)),
             dma,
             dma,
-        ],
-        compiler_params=pltpu.CompilerParams(collective_id=slots, has_side_effects=True, vmem_limit_bytes=56 << 20),
+        ]
+        + temps,
+        compiler_params=pltpu.CompilerParams(collective_id=slots, has_side_effects=True, vmem_limit_bytes=60 << 20),
         name=f"tree_{slots}",
-    )(parent, carry, own)
+    )(parent, carry, own, *inner)
 
 
 FEW = 7
 ALL = 13
-
-
-def busiest(parent):
-    nodes = NX * NZ
-    i = jnp.arange(nodes, dtype=jnp.int32)
-    near = (parent[None, :] == i[:, None]) | (parent < 0)[:, None]
-    up, down = arms(near, (i[None, :] - i[:, None]) & (NZ - 1))
-    e = jnp.arange(NZ, dtype=jnp.int32)[None, :]
-    used = (((e - i[:, None]) & (NZ - 1)) < up) | (((i[:, None] - 1 - e) & (NZ - 1)) < down)
-    return jnp.max(jnp.sum(used.astype(jnp.int32), axis=0))
 
 
 def body(inputs, dt_raw, b_proj, c_proj, a_log, dt_bias, skip, grad_out, parent, children):
     heads = a_log.shape[0]
     groups = b_proj.shape[2] // STATE
     per = heads // BLOCK // groups
+    dps = lax.axis_size("dp")
     x, dy, raw, b, c = inputs[0], grad_out[0], dt_raw[0], b_proj[0], c_proj[0]
-    alog, bias, skips = a_log[:, None], dt_bias[:, None], skip[:, None]
-    few = lax.pmax(busiest(parent), "dp") <= FEW
-    own, carry, xt, dyt = summaries(x, dy, raw, b, c, alog, bias, per)
-    inner = inner_grads(dy, raw, b, c, alog, bias, skips, xt, dyt, per)
-    both = lax.cond(few, functools.partial(tree, FEW), functools.partial(tree, ALL), parent, carry, own)
-    gx, gdt, gb, gc = final_grads(raw, b, c, alog, bias, xt, dyt, both, inner, per)
+    alog, bias = a_log[:, None], dt_bias[:, None]
+    own, carry, xt, dyt, rise, fall = summaries(x, dy, raw, b, c, alog, bias, per)
+    both, most, *inner = tree(FEW, dps, parent, carry, own, (skip, dy, b, c, xt, dyt, rise, fall))
+
+    def ending(states):
+        return final_grads(raw, b, c, alog, bias, xt, dyt, states, inner, per)
+
+    gx, gdt, gb, gc = lax.cond(
+        most[0, 0] < FEW + 0.5,
+        lambda: tuple(ending(both)),
+        lambda: tuple(ending(tree(ALL, dps, parent, carry, own)[0])),
+    )
     return gx[None], gdt[None], gb[None], gc[None]
 
 

time: 188 us -> 161 us (0.86)
  Pallas kernels: 163 us -> 154 us
  blocking collectives: 8.56 us -> 0 us
  local copies, waits for them, and re-layouts: 13.3 us -> 5.35 us
    pallas_call x2 -> x1, Pallas kernels: 148 us -> 133 us  [tree(): pl.pallas_call(functools.partial(tree_kernel, slots, dps, per), in_specs=...]
    unnamed x34 -> x12, local copies, waits for them, and re-layouts: 11.7 us -> 0.03 us
    pmax x1 -> x0, blocking collectives: 8.56 us -> none  [body(): few = lax.pmax(busiest(parent), 'dp') <= FEW]
    pallas_call x1, Pallas kernels: 6.85 us -> 10.1 us  [summaries(): pl.pallas_call(first_kernel, grid=(heads // BLOCK,), in_specs=[s['nat'],...]
    pallas_call x1, Pallas kernels: 7.63 us -> 10.7 us  [final_grads(): pl.pallas_call(functools.partial(last_kernel, per), grid=(heads // BLOCK,...]
where the time goes in v3:
time: 161 us; the launch traced here: 160 us
  Pallas kernels  154 us (96%)
  local copies, waits for them, and re-layouts  5.35 us (3%)
    pallas_call x1, Pallas kernels, tree(): pl.pallas_call(functools.partial(tree_kernel, slots, dps, per), in_specs=...  133 us
    pallas_call x1, Pallas kernels, final_grads(): pl.pallas_call(functools.partial(last_kernel, per), grid=(heads // BLOCK,...  10.7 us
    pallas_call x1, Pallas kernels, summaries(): pl.pallas_call(first_kernel, grid=(heads // BLOCK,), in_specs=[s['nat'],...  10.1 us

profile of v3, /device:TPU:16, one launch (start us, length us, event | category | flops | bytes accessed | tf_op | source)
XLA Modules:
  0.0 160.3 jit_solution(2887423693524447883)
XLA Ops:
  0.6 1.4 copy.13.alog_ref
  2.0 1.4 copy.14.bias_ref
  3.3 0.0 copy-start
  3.4 0.0 copy-start.1
  3.4 0.0 copy-start.5
  3.4 10.1 %summaries.1 = (f32[64,2,64,128]{3,2,1,0:T(8,128)}, f32[64,128]{1,0:T(8,128)S(1)}, bf16[4096,256]{1,0:T(8,128)(2,1)S(1)}, bf16[4096,256]{1,0:T(8,128)(2,1)}, f32...) custom-call(bf16[256,4096]{1,0:T(8,128)(2,1)} %bitcast.14, bf16[256,4096]{1,0:T(8,128)(2,1)} %bitcast.12, f32[64,256]{1,0:T(8,128)} %bitcast.23, ...), custom_call_target="tpu_custom_call" | custom-call | tf_op jit(solution)/shard_map/summaries/pallas_call | solution.py:207
  13.5 0.0 copy-done
  13.5 0.0 copy-done.1
  13.5 0.0 copy-done.5
  13.5 0.0 copy-start.2
  13.5 0.0 copy-start.3
  13.5 0.0 copy-start.4
  13.6 132.7 %tree_7.1 = (f32[64,2,64,128]{3,2,1,0:T(8,128)}, f32[8,128]{1,0:T(8,128)}, f32[4096,256]{1,0:T(8,128)}, f32[32,2,256]{2,1,0:T(2,128)S(1)}, f32[32,2,256]{2,1,0:T...) custom-call(s32[32]{0:T(128)S(1)} %copy-done.5, f32[64,128]{1,0:T(8,128)S(1)} %get-tuple-element.122.carry_ref, ...), custom_call_target="tpu_custom_call" | custom-call | tf_op jit(solution)/shard_map/tree_7/pallas_call | solution.py:562
  146.3 1.2 slice.3
  148.1 0.0 copy-done.2
  148.2 0.0 copy-done.3
  148.2 0.0 copy-done.4
  148.2 12.1 %conditional.1 = ((bf16[256,4096]{1,0:T(8,128)(2,1)}, f32[64,256]{1,0:T(8,128)}, f32[256,256]{1,0:T(8,128)}, f32[256,256]{1,0:T(8,128)})) conditional(s32[]{:T(128)} %bitcast.7, (s32[32]{0:T(128)S(1)}, f32[64,128]{1,0:T(8,128)S(1)}, f32[64,2,64,128]{3,2,1,0:T(8,128)}, f32[64,256]{1,0:T(8,128)S(1)}, bf16[256,256]{1,0:T(8,128)(2,1)S(1)}, ...), branch_computations={%region_0.0_spmd.clone, %region_1.0_spmd.clone} | conditional | bytes 1032 | solution.py:618
  148.2 0.7 copy.18.bias_ref
  148.9 0.7 copy.17.alog_ref
  149.6 10.7 %final_grads.3 = (bf16[256,4096]{1,0:T(8,128)(2,1)}, f32[64,256]{1,0:T(8,128)}, f32[256,256]{1,0:T(8,128)}, f32[256,256]{1,0:T(8,128)}) custom-call(f32[64,256]{1,0:T(8,128)S(1)} %get-tuple-element.158.raw_ref, bf16[256,256]{1,0:T(8,128)(2,1)S(1)} %get-tuple-element.159.b_ref, bf16[256,256]{1,0:T(8,128)(2,1)S(1)} %get-tuple-element.160.c_ref, ...), custom_call_target="tpu_custom_call" | custom-call | tf_op jit(solution)/shard_map/cond/branch_1_fun/final_grads/pallas_call | solution.py:229
Async XLA Ops:
  3.3 10.1 %copy-start = (bf16[1,256,256]{2,1,0:T(8,128)(2,1)S(1)}, bf16[1,256,256]{2,1,0:T(8,128)(2,1)}, u32[]{:S(2)}) copy-start(bf16[1,256,256]{2,1,0:T(8,128)(2,1)} %param.14) | copy-start | bytes 393220
  3.4 10.1 %copy-start.1 = (bf16[1,256,256]{2,1,0:T(8,128)(2,1)S(1)}, bf16[1,256,256]{2,1,0:T(8,128)(2,1)}, u32[]{:S(2)}) copy-start(bf16[1,256,256]{2,1,0:T(8,128)(2,1)} %param.15) | copy-start | bytes 393220
  3.4 10.2 %copy-start.5 = (s32[32]{0:T(128)S(1)}, s32[32]{0:T(128)}, u32[]{:S(2)}) copy-start(s32[32]{0:T(128)} %parent_ref.1) | copy-start | bytes 388
  13.5 134.6 %copy-start.2 = (f32[1,64,256]{2,1,0:T(8,128)S(1)}, f32[1,64,256]{2,1,0:T(8,128)}, u32[]{:S(2)}) copy-start(f32[1,64,256]{2,1,0:T(8,128)} %param.13) | copy-start | bytes 196612
  13.5 134.6 %copy-start.3 = (f32[64]{0:T(128)S(1)}, f32[64]{0:T(128)}, u32[]{:S(2)}) copy-start(f32[64]{0:T(128)} %param.16) | copy-start | bytes 772
  13.5 134.6 %copy-start.4 = (f32[64]{0:T(128)S(1)}, f32[64]{0:T(128)}, u32[]{:S(2)}) copy-start(f32[64]{0:T(128)} %param.17) | copy-start | bytes 772

commit v4 on v3

--- a/solution.py
+++ b/solution.py
@@ -9,7 +9,6 @@
 
 HEAD_DIM = 64
 STATE = 128
-BLOCK = 8
 NX = 4
 NZ = 8
 ARM = 4
@@ -38,13 +37,6 @@
     return jnp.where(r >= c if lower else r <= c, 1.0, 0.0).astype(BF16)
 
 
-def rates(raw, alog, bias):
-    v = raw + bias
-    rate = jnp.maximum(v, 0.0) + jnp.log1p(jnp.exp(-jnp.abs(v)))
-    cum = prefix(-jnp.exp(alog) * rate, triangle(raw.shape[1], False))
-    return rate, cum
-
-
 def spread(rows, flat):
     h, t = rows.shape
     return (flat.astype(F32).reshape(h, -1, t) * rows[:, None, :]).reshape(flat.shape)
@@ -54,44 +46,65 @@
     return flat.reshape(heads, -1, flat.shape[1]).sum(axis=1)
 
 
-def first_kernel(x_ref, dy_ref, raw_ref, b_ref, c_ref, alog_ref, bias_ref, own_ref, carry_ref, xt_ref, dyt_ref, rise_ref, fall_ref):
-    rate, cum = rates(raw_ref[...], alog_ref[...], bias_ref[...])
-    last = cum[:, -1:]
-    tail = jnp.exp(last - cum) * rate
-    growth = jnp.exp(cum)
-    xt = x_ref[...].T
-    dyt = dy_ref[...].T
-    xt_ref[...] = xt
-    dyt_ref[...] = dyt
-    end = dot(spread(tail, xt).astype(BF16), b_ref[...])
-    pull = dot(spread(growth, dyt).astype(BF16), c_ref[...])
-    own_ref[:, 0] = end.reshape(BLOCK, HEAD_DIM, STATE)
-    own_ref[:, 1] = pull.reshape(BLOCK, HEAD_DIM, STATE)
-    carry_ref[...] = jnp.broadcast_to(jnp.exp(last), carry_ref.shape)
+def scalars(ref, shape):
+    row = lax.broadcasted_iota(jnp.int32, shape, 0)
+    out = jnp.zeros(shape, F32)
+    for h in range(shape[0]):
+        out = jnp.where(row == h, ref[h], out)
+    return out[:, :1]
+
+
+def prepare(slots, alog_ref, bias_ref, raw_ref, b_ref, c_ref, rate_s, slope_s, rise_s, fall_s, tail_s, growth_s, ones_s, score, summed, sumb, sumc):
+    heads, t = raw_ref.shape
+    v = raw_ref[...] + scalars(bias_ref, (heads, STATE))
+    rate = jnp.maximum(v, 0.0) + jnp.log1p(jnp.exp(-jnp.abs(v)))
+    rate_s[...] = rate
+    slope_s[...] = 1.0 / (1.0 + jnp.exp(-v))
+    cum = prefix(-jnp.exp(scalars(alog_ref, (heads, STATE))) * rate, triangle(t, False))
+    ones_s[...] = triangle(t, True)
     rise = cum.T
     fall = jnp.log(rate) - cum
-    for i in range(BLOCK // 2):
-        rise_ref[i] = rise[:, 2 * i : 2 * i + 2]
-        fall_ref[i] = fall[2 * i : 2 * i + 2]
-
-
-def inner_pair(pair, per, skip_ref, dy_ref, b_ref, c_ref, xt_ref, dyt_ref, rise_ref, fall_ref, dx_ref, row_ref, col_ref, dbt_ref, dct_ref, score, summed):
+    tail = jnp.exp(cum[:, -1:] - cum) * rate
+    growth = jnp.exp(cum)
+    for i in range(heads // 2):
+        two = slice(2 * i, 2 * i + 2)
+        rise_s[i] = rise[:, two]
+        fall_s[i] = fall[two]
+        tail_s[i] = tail[two]
+        growth_s[i] = growth[two]
+    for g in range(score.shape[0]):
+        group = slice(g * STATE, (g + 1) * STATE)
+        score[g] = dot(c_ref[:, group], b_ref[:, group], 1, 1)
+    summed[...] = jnp.zeros_like(summed)
+    sumb[...] = jnp.zeros_like(sumb)
+    sumc[...] = jnp.zeros_like(sumc)
+    return jnp.exp(rise[t - 1 :, :])
+
+
+def columns(index, width):
+    return pl.ds(pl.multiple_of(index * width, width), width)
+
+
+def summary_pair(pair, group, x_ref, dy_ref, b_ref, c_ref, xt_s, dyt_s, tail_s, growth_s):
+    mine = columns(pair, 2 * HEAD_DIM)
+    xt = x_ref[:, mine].T
+    dyt = dy_ref[:, mine].T
+    xt_s[pair] = xt
+    dyt_s[pair] = dyt
+    end = dot(spread(tail_s[pair], xt).astype(BF16), b_ref[:, columns(group, STATE)])
+    pull = dot(spread(growth_s[pair], dyt).astype(BF16), c_ref[:, columns(group, STATE)])
+    return end.reshape(2, HEAD_DIM, STATE), pull.reshape(2, HEAD_DIM, STATE)
+
+
+def inner_pair(pair, group, skip_ref, dy_ref, xt_s, dyt_s, rise_s, fall_s, dx_s, row_s, col_s, score, summed):
     t = dy_ref.shape[0]
     half = t // 2
     both = 2 * HEAD_DIM
-    group = pl.ds(pl.multiple_of(pair // per * STATE, STATE), STATE)
-
-    @pl.when(lax.rem(pair, per) == 0)
-    def _():
-        score[...] = dot(c_ref[:, group], b_ref[:, group], 1, 1)
-        summed[...] = jnp.zeros_like(summed)
-
-    mine = pl.ds(pl.multiple_of(pair * both, both), both)
-    rise = rise_ref[pair]
-    fall = fall_ref[pair]
-    xpair = xt_ref[mine, :]
-    dypair = dyt_ref[mine, :]
-    dycols = dy_ref[:, mine]
+    rise = rise_s[pair]
+    fall = fall_s[pair]
+    xpair = xt_s[pair]
+    dypair = dyt_s[pair]
+    dycols = dy_ref[:, columns(pair, both)]
     causal = lax.broadcasted_iota(jnp.int32, (half, half), 0) >= lax.broadcasted_iota(jnp.int32, (half, half), 1)
     where_x = lax.broadcasted_iota(jnp.int32, (both, t), 0) // HEAD_DIM
     lefts, downs, outs = [], [], []
@@ -107,9 +120,9 @@
             if a == b:
                 gap = jnp.where(causal, gap, -1e30)
             decay = jnp.exp(gap)
-            mix = decay * score[rows, cols]
+            mix = decay * score[group, rows, cols]
             dmix = dot(dycols[rows], xhead[:, cols])
-            summed[rows, cols] += dmix * decay
+            summed[group, rows, cols] += dmix * decay
             parts[a, b] = (mix.astype(BF16), dmix * mix)
         q0, q1, q2 = parts[0, 0][1], parts[1, 0][1], parts[1, 1][1]
         downs.append(
@@ -122,125 +135,50 @@
         outs.append(
             jnp.concatenate([dot(dyh, left), dot(dyh[:, half:], parts[1, 1][0])], axis=1) + skip * dyh.astype(F32)
         )
-    dx_ref[mine, :] = jnp.concatenate(outs, axis=0)
-    col_ref[pair] = jnp.concatenate(downs, axis=0)
-    row_ref[pair] = jnp.concatenate(lefts, axis=1).T
-
-    @pl.when(lax.rem(pair, per) == per - 1)
-    def _():
-        r = lax.broadcasted_iota(jnp.int32, (t, t), 0)
-        c = lax.broadcasted_iota(jnp.int32, (t, t), 1)
-        low = jnp.where(r >= c, summed[...], 0.0).astype(BF16)
-        dbt_ref[group, :] = dot(c_ref[:, group], low, 0, 0)
-        dct_ref[group, :] = dot(b_ref[:, group], low, 0, 1)
-
-
-def last_kernel(per, raw_ref, b_ref, c_ref, alog_ref, bias_ref, xt_ref, dyt_ref, both_ref, dx_ref, row_ref, col_ref, dbt_ref, dct_ref, gx_ref, gdt_ref, gb_ref, gc_ref, sumb, sumc):
-    step = pl.program_id(0)
-    t = raw_ref.shape[1]
-
-    @pl.when(step % per == 0)
-    def _():
-        sumb[...] = dbt_ref[...]
-        sumc[...] = dct_ref[...]
-
-    v = raw_ref[...] + bias_ref[...]
-    rate, cum = rates(raw_ref[...], alog_ref[...], bias_ref[...])
-    last = cum[:, -1:]
-    growth = jnp.exp(cum)
-    tail = jnp.exp(last - cum) * rate
-    start = both_ref[:, 0].reshape(BLOCK * HEAD_DIM, STATE)
-    grad = both_ref[:, 1].reshape(BLOCK * HEAD_DIM, STATE)
-    inner = jnp.sum(fold(start * grad, BLOCK), axis=1, keepdims=True)
+    dx_s[pair] = jnp.concatenate(outs, axis=0)
+    col_s[pair] = jnp.concatenate(downs, axis=0)
+    row_s[pair] = jnp.concatenate(lefts, axis=1).T
+
+
+def final_pair(pair, group, b_ref, c_ref, states, xt_s, dyt_s, tail_s, growth_s, dx_s, row_s, col_s, sumb, sumc, gx_ref):
+    two = pl.ds(2 * pair, 2)
+    start = states[two, 0].reshape(2 * HEAD_DIM, STATE)
+    grad = states[two, 1].reshape(2 * HEAD_DIM, STATE)
+    tail = tail_s[pair]
+    growth = growth_s[pair]
+    inner = jnp.sum(fold(start * grad, 2), axis=1, keepdims=True)
     start_low = start.astype(BF16)
     grad_low = grad.astype(BF16)
-    xt = xt_ref[...]
-    dyt = dyt_ref[...]
-    pulled = dot(grad_low, b_ref[...], 1, 1)
-    z = fold(xt.astype(F32) * pulled, BLOCK) * tail
-    gx_ref[...] = (dx_ref[...] + spread(tail, pulled)).astype(BF16).T
-    sumb[...] += dot(grad_low, spread(tail, xt).astype(BF16), 0, 0)
-    carried = dot(start_low, c_ref[...], 1, 1)
-    g = fold(dyt.astype(F32) * carried, BLOCK) * growth
-    sumc[...] += dot(start_low, spread(growth, dyt).astype(BF16), 0, 0)
-    col = jnp.concatenate([col_ref[i] for i in range(BLOCK // 2)], axis=0)
-    row = jnp.concatenate([row_ref[i] for i in range(BLOCK // 2)], axis=0)
-    dcum = row - col + g - z
+    xt = xt_s[pair]
+    dyt = dyt_s[pair]
+    own = columns(group, STATE)
+    pulled = dot(grad_low, b_ref[:, own], 1, 1)
+    z = fold(xt.astype(F32) * pulled, 2) * tail
+    gx_ref[:, columns(pair, 2 * HEAD_DIM)] = (dx_s[pair] + spread(tail, pulled)).astype(BF16).T
+    sumb[group] += dot(grad_low, spread(tail, xt).astype(BF16), 0, 0)
+    carried = dot(start_low, c_ref[:, own], 1, 1)
+    g = fold(dyt.astype(F32) * carried, 2) * growth
+    sumc[group] += dot(start_low, spread(growth, dyt).astype(BF16), 0, 0)
+    col = col_s[pair]
     at_end = jnp.sum(z, axis=1, keepdims=True) + growth[:, -1:] * inner
-    dlog = prefix(dcum, triangle(t, True)) + at_end
-    slope = 1.0 / (1.0 + jnp.exp(-v))
-    gdt_ref[...] = ((col + z) / rate - jnp.exp(alog_ref[...]) * dlog) * slope
-
-    @pl.when(step % per == per - 1)
-    def _():
-        gb_ref[...] = sumb[...].T
-        gc_ref[...] = sumc[...].T
-
-
-def specs(per, t):
-    flat = pl.BlockSpec((BLOCK * HEAD_DIM, t), lambda i: (i, 0))
-    return {
-        "nat": pl.BlockSpec((t, BLOCK * HEAD_DIM), lambda i: (0, i)),
-        "rows": pl.BlockSpec((BLOCK, t), lambda i: (i, 0)),
-        "group": pl.BlockSpec((t, STATE), lambda i: (0, i // per)),
-        "one": pl.BlockSpec((BLOCK, 1), lambda i: (i, 0)),
-        "flat": flat,
-        "state": pl.BlockSpec((BLOCK, 2, HEAD_DIM, STATE), lambda i: (i, 0, 0, 0)),
-        "lane": pl.BlockSpec((BLOCK, STATE), lambda i: (i, 0)),
-        "rise": pl.BlockSpec((BLOCK // 2, t, 2), lambda i: (i, 0, 0)),
-        "pairs": pl.BlockSpec((BLOCK // 2, 2, t), lambda i: (i, 0, 0)),
-        "groupt": pl.BlockSpec((STATE, t), lambda i: (i // per, 0)),
-    }
-
-
-def params(mib):
-    return pltpu.CompilerParams(vmem_limit_bytes=mib << 20)
-
-
-def sds(shape, kind=F32):
-    return jax.ShapeDtypeStruct(shape, kind)
-
-
-def summaries(x, dy, raw, b, c, alog, bias, per):
-    heads, t = raw.shape
-    s = specs(per, t)
-    return pl.pallas_call(
-        first_kernel,
-        grid=(heads // BLOCK,),
-        in_specs=[s["nat"], s["nat"], s["rows"], s["group"], s["group"], s["one"], s["one"]],
-        out_specs=[s["state"], s["lane"], s["flat"], s["flat"], s["rise"], s["pairs"]],
-        out_shape=[
-            sds((heads, 2, HEAD_DIM, STATE)),
-            sds((heads, STATE)),
-            sds((heads * HEAD_DIM, t), BF16),
-            sds((heads * HEAD_DIM, t), BF16),
-            sds((heads // 2, t, 2)),
-            sds((heads // 2, 2, t)),
-        ],
-        compiler_params=params(60),
-        name="summaries",
-    )(x, dy, raw, b, c, alog, bias)
-
-
-def final_grads(raw, b, c, alog, bias, xt, dyt, both, inner, per):
-    heads, t = raw.shape
-    s = specs(per, t)
-    groups = heads // BLOCK // per
-    return pl.pallas_call(
-        functools.partial(last_kernel, per),
-        grid=(heads // BLOCK,),
-        in_specs=[s["rows"], s["group"], s["group"], s["one"], s["one"], s["flat"], s["flat"], s["state"], s["flat"], s["pairs"], s["pairs"], s["groupt"], s["groupt"]],
-        out_specs=[s["nat"], s["rows"], s["group"], s["group"]],
-        out_shape=[
-            sds((t, heads * HEAD_DIM), BF16),
-            sds((heads, t)),
-            sds((t, groups * STATE)),
-            sds((t, groups * STATE)),
-        ],
-        scratch_shapes=[pltpu.VMEM((STATE, t), F32), pltpu.VMEM((STATE, t), F32)],
-        compiler_params=params(60),
-        name="final_grads",
-    )(raw, b, c, alog, bias, xt, dyt, both, *inner)
+    lane = lax.broadcasted_iota(jnp.int32, z.shape, 1)
+    row_s[pair] = row_s[pair] - col + g - z + jnp.where(lane == z.shape[1] - 1, at_end, 0.0)
+    col_s[pair] = col + z
+
+
+def finish(alog_ref, b_ref, c_ref, rate_s, slope_s, ones_s, row_s, col_s, summed, sumb, sumc, gdt_ref, gb_ref, gc_ref):
+    heads, t = rate_s.shape
+    dcum = jnp.concatenate([row_s[i] for i in range(heads // 2)], axis=0)
+    dlog_rate = jnp.concatenate([col_s[i] for i in range(heads // 2)], axis=0)
+    dlog = prefix(dcum, ones_s[...])
+    gdt_ref[...] = (dlog_rate / rate_s[...] - jnp.exp(scalars(alog_ref, (heads, STATE))) * dlog) * slope_s[...]
+    r = lax.broadcasted_iota(jnp.int32, (t, t), 0)
+    c = lax.broadcasted_iota(jnp.int32, (t, t), 1)
+    for g in range(summed.shape[0]):
+        group = slice(g * STATE, (g + 1) * STATE)
+        low = jnp.where(r >= c, summed[g], 0.0).astype(BF16)
+        gb_ref[:, group] = (sumb[g] + dot(c_ref[:, group], low, 0, 0)).T
+        gc_ref[:, group] = (sumc[g] + dot(b_ref[:, group], low, 0, 1)).T
 
 
 def arms(near, pick):
@@ -253,21 +191,19 @@
     return jnp.where(both & (up >= down), ARM, up), jnp.where(both & (up < down), ARM, down)
 
 
-def tree_kernel(slots, dps, per, parent_ref, carry_ref, own_ref, *refs):
-    ins, refs = (refs[:8], refs[8:]) if per else ((), refs)
-    (both_ref, most_ref), refs = refs[:2], refs[2:]
-    outs, refs = (refs[:5], refs[5:]) if per else ((), refs)
-    tree_steps(slots, dps, per, parent_ref, carry_ref, own_ref, ins, both_ref, most_ref, outs, refs[25:], *refs[:25])
-
-
-def tree_steps(slots, dps, per, parent_ref, carry_ref, own_ref, ins, both_ref, most_ref, outs, temps, counts, count_send, count_recv, xin, extra, got, put, res, crow, carried, scale, relay, local, remote, here,
-                own_sem, in_send, in_recv, z_send, z_recv, out_send, out_recv, out_own, carry_send, carry_recv):
+def whole_kernel(slots, dps, parent_ref, alog_ref, bias_ref, skip_ref, x_ref, dy_ref, raw_ref, b_ref, c_ref,
+                 gx_ref, gdt_ref, gb_ref, gc_ref, most_ref,
+                 rate_s, slope_s, rise_s, fall_s, tail_s, growth_s, ones_s, score, summed, sumb, sumc, xt_s, dyt_s, dx_s, row_s, col_s, own_ref, both_ref,
+                 counts, count_send, count_recv, xin, extra, got, put, res, crow, carried, scale, relay, local, remote, here,
+                 in_send, in_recv, z_send, z_recv, out_send, out_recv, out_own, carry_send, carry_recv):
     nodes = NX * NZ
     part = own_ref.shape[0] // NX
     half = HEAD_DIM // 2
     chunks = part * 2
     rounds = chunks + LAG * (ARM - 1)
-    ahead = 3
+    pairs = own_ref.shape[0] // 2
+    groups = score.shape[0]
+    first = 2 * NX
     me = lax.axis_index("leaf")
     x, z = me // NZ, lax.rem(me, NZ)
 
@@ -287,8 +223,32 @@
         pl.semaphore_signal(barrier, inc=1, device_id={"leaf": lax.rem(me + k, nodes)}, device_id_type=MESH)
 
     crow[...] = jnp.zeros_like(crow)
-    crow[0, :, : carry_ref.shape[0]] = carry_ref[...].T[0:1, :]
+    crow[0, :, : own_ref.shape[0]] = prepare(
+        slots, alog_ref, bias_ref, raw_ref, b_ref, c_ref, rate_s, slope_s, rise_s, fall_s, tail_s, growth_s, ones_s, score, summed, sumb, sumc
+    )
     got[:, 0:LAG] = jnp.zeros((2, LAG) + got.shape[2:], F32)
+
+    def place(index):
+        side = lax.rem(index, NX)
+        pair = side * (pairs // NX) + index // NX
+        return pair, side, pair // (pairs // groups)
+
+    def summary(index):
+        pair, side, group = place(index)
+        end, pull = summary_pair(pair, group, x_ref, dy_ref, b_ref, c_ref, xt_s, dyt_s, tail_s, growth_s)
+        own_ref[pl.ds(2 * pair, 2), 0] = end
+        own_ref[pl.ds(2 * pair, 2), 1] = pull
+
+        @pl.when(side == x)
+        def _():
+            hd = pl.ds(2 * (index // NX), 2)
+            xin[x, hd, 0] = end
+            xin[x, hd, 1] = pull
+
+    @pl.loop(0, first)
+    def _(index):
+        summary(index)
+
     pl.semaphore_wait(barrier, nodes + dps - 2)
 
     def in_copy(hd, k):
@@ -305,8 +265,6 @@
         for k in range(1, NX):
             in_copy(hd, k).start()
 
-    own_copy = pltpu.make_async_copy(own_ref.at[pl.ds(x * part, part)], xin.at[x], own_sem)
-    own_copy.start()
     start_in(0)
 
     def carry_copy(k):
@@ -323,7 +281,7 @@
     def _(k):
         carry_copy(k).start()
 
-    for hd in range(1, ahead):
+    for hd in range(1, 2 * first // NX):
         start_in(hd)
 
     lanes = 128
@@ -411,8 +369,6 @@
     for k in range(NX):
         row = jnp.sum(jnp.where(is_root, 0.0, wants[k] * decays), axis=0, keepdims=True)
         scale[k] = jnp.broadcast_to(row, (lanes, lanes)).T[: scale.shape[1], None, :]
-    own_copy.wait()
-
     def z_copy(way, r):
         to = lax.rem(z + (1 if way == 0 else NZ - 1), NZ)
         return pltpu.make_async_remote_copy(
@@ -443,7 +399,9 @@
 
     last = LAG * ARM
 
-    @pl.loop(0, chunks + last)
+    late = last + 2 * NX - 2
+
+    @pl.loop(0, pairs + late)
     def _(r):
         @pl.when((r >= LAG) & (r < rounds + LAG))
         def _():
@@ -453,10 +411,6 @@
         @pl.when((lax.rem(r, 2) == 0) & (r < chunks))
         def _():
             hd = r // 2
-
-            @pl.when(hd + ahead < part)
-            def _():
-                start_in(hd + ahead)
 
             for k in range(1, NX):
                 in_copy(hd, k).wait_recv()
@@ -488,7 +442,7 @@
                 put[way, lax.rem(r, 3)] = acc
                 z_copy(way, r).start()
 
-        @pl.when(r >= last)
+        @pl.when((r >= last) & (r < chunks + last))
         def _():
             c = r - last
             hd = c // 2
@@ -516,12 +470,36 @@
                     out_copy(hd, k).start()
                 own_out(hd).start()
 
-        if per:
-
-            @pl.when(r < ins[0].shape[0] // 2)
+        @pl.when(r + first < pairs)
+        def _():
+            summary(r + first)
+
+            @pl.when(lax.rem(r + first, NX) == NX - 1)
             def _():
-                inner_pair(r, per, *ins, *outs, *temps)
-
+                start_in(2 * ((r + first) // NX))
+                start_in(2 * ((r + first) // NX) + 1)
+
+        @pl.when(r < pairs)
+        def _():
+            pair, side, group = place(r)
+            inner_pair(pair, group, skip_ref, dy_ref, xt_s, dyt_s, rise_s, fall_s, dx_s, row_s, col_s, score, summed)
+
+        @pl.when(r >= late)
+        def _():
+            index = r - late
+
+            @pl.when(lax.rem(index, NX) == 0)
+            def _():
+                for one_of in range(2):
+                    hd = 2 * (index // NX) + one_of
+                    for k in range(1, NX):
+                        out_copy(hd, k).wait_recv()
+                    own_out(hd).wait()
+
+            pair, side, group = place(index)
+            final_pair(pair, group, b_ref, c_ref, both_ref, xt_s, dyt_s, tail_s, growth_s, dx_s, row_s, col_s, sumb, sumc, gx_ref)
+
+    finish(alog_ref, b_ref, c_ref, rate_s, slope_s, ones_s, row_s, col_s, summed, sumb, sumc, gdt_ref, gb_ref, gc_ref)
     for k in range(1, dps):
         count_copy(k).wait()
     most = counts[0]
@@ -536,36 +514,55 @@
     def _(hd):
         for k in range(1, NX):
             in_copy(hd, k).wait_send()
-            out_copy(hd, k).wait()
-        own_out(hd).wait()
-
-
-def tree(slots, dps, parent, carry, own, inner=()):
-    heads = own.shape[0]
+            out_copy(hd, k).wait_send()
+
+
+def sds(shape, kind=F32):
+    return jax.ShapeDtypeStruct(shape, kind)
+
+
+def whole(slots, dps, parent, alog, bias, skip, x, dy, raw, b, c):
+    heads, t = raw.shape
+    pairs = heads // 2
+    groups = b.shape[1] // STATE
     part = heads // NX
     half = HEAD_DIM // 2
     rounds = part * 2 + LAG * (ARM - 1)
     dma = pltpu.SemaphoreType.DMA
     vmem = pl.BlockSpec(memory_space=pltpu.VMEM)
-    outs, temps, per = [], [], 0
-    if inner:
-        t, groups = inner[1].shape[0], inner[2].shape[1] // STATE
-        per = heads // 2 // groups
-        outs = [
-            sds((heads * HEAD_DIM, t)),
-            sds((heads // 2, 2, t)),
-            sds((heads // 2, 2, t)),
-            sds((groups * STATE, t)),
-            sds((groups * STATE, t)),
-        ]
-        temps = [pltpu.VMEM((t, t), F32), pltpu.VMEM((t, t), F32)]
+    smem = pl.BlockSpec(memory_space=pltpu.SMEM)
+    rows = pltpu.VMEM((pairs, 2, t), F32)
+    turned = pltpu.VMEM((pairs, 2 * HEAD_DIM, t), BF16)
     return pl.pallas_call(
-        functools.partial(tree_kernel, slots, dps, per),
-        in_specs=[pl.BlockSpec(memory_space=pltpu.SMEM), vmem, pl.BlockSpec(memory_space=pl.ANY)]
-        + ([pl.BlockSpec(memory_space=pltpu.SMEM)] + [vmem] * 7 if inner else []),
-        out_specs=[pl.BlockSpec(memory_space=pl.ANY), vmem] + [vmem] * len(outs),
-        out_shape=[sds(own.shape), sds((8, STATE))] + outs,
+        functools.partial(whole_kernel, slots, dps),
+        in_specs=[smem] * 4 + [vmem] * 5,
+        out_specs=[vmem] * 5,
+        out_shape=[
+            sds((t, heads * HEAD_DIM), BF16),
+            sds((heads, t)),
+            sds((t, groups * STATE)),
+            sds((t, groups * STATE)),
+            sds((8, STATE)),
+        ],
         scratch_shapes=[
+            pltpu.VMEM((heads, t), F32),
+            pltpu.VMEM((heads, t), F32),
+            pltpu.VMEM((pairs, t, 2), F32),
+            rows,
+            rows,
+            rows,
+            pltpu.VMEM((t, t), BF16),
+            pltpu.VMEM((groups, t, t), F32),
+            pltpu.VMEM((groups, t, t), F32),
+            pltpu.VMEM((groups, STATE, t), F32),
+            pltpu.VMEM((groups, STATE, t), F32),
+            turned,
+            turned,
+            pltpu.VMEM((pairs, 2 * HEAD_DIM, t), F32),
+            rows,
+            rows,
+            pltpu.VMEM((heads, 2, HEAD_DIM, STATE), F32),
+            pltpu.VMEM((heads, 2, HEAD_DIM, STATE), F32),
             pltpu.VMEM((dps, 1, STATE), F32),
             dma((dps,)),
             dma((dps,)),
@@ -581,7 +578,6 @@
             pltpu.VMEM((2, NX, slots, 1, STATE), F32),
             pltpu.VMEM((2, ARM, NX + 1, slots, 1, STATE), F32),
             pltpu.VMEM((NX, NX + 1, 1, STATE), F32),
-            dma,
             dma((part, NX - 1)),
             dma((part, NX - 1)),
             dma((2, 3)),
@@ -591,11 +587,10 @@
             dma((part,)),
             dma,
             dma,
-        ]
-        + temps,
-        compiler_params=pltpu.CompilerParams(collective_id=slots, has_side_effects=True, vmem_limit_bytes=60 << 20),
-        name=f"tree_{slots}",
-    )(parent, carry, own, *inner)
+        ],
+        compiler_params=pltpu.CompilerParams(collective_id=slots, has_side_effects=True, vmem_limit_bytes=62 << 20),
+        name=f"whole_{slots}",
+    )(parent, alog, bias, skip, x, dy, raw, b, c)
 
 
 FEW = 7
@@ -603,24 +598,11 @@
 
 
 def body(inputs, dt_raw, b_proj, c_proj, a_log, dt_bias, skip, grad_out, parent, children):
-    heads = a_log.shape[0]
-    groups = b_proj.shape[2] // STATE
-    per = heads // BLOCK // groups
+    given = (parent, a_log, dt_bias, skip, inputs[0], grad_out[0], dt_raw[0], b_proj[0], c_proj[0])
     dps = lax.axis_size("dp")
-    x, dy, raw, b, c = inputs[0], grad_out[0], dt_raw[0], b_proj[0], c_proj[0]
-    alog, bias = a_log[:, None], dt_bias[:, None]
-    own, carry, xt, dyt, rise, fall = summaries(x, dy, raw, b, c, alog, bias, per)
-    both, most, *inner = tree(FEW, dps, parent, carry, own, (skip, dy, b, c, xt, dyt, rise, fall))
-
-    def ending(states):
-        return final_grads(raw, b, c, alog, bias, xt, dyt, states, inner, per)
-
-    gx, gdt, gb, gc = lax.cond(
-        most[0, 0] < FEW + 0.5,
-        lambda: tuple(ending(both)),
-        lambda: tuple(ending(tree(ALL, dps, parent, carry, own)[0])),
-    )
-    return gx[None], gdt[None], gb[None], gc[None]
+    *grads, most = whole(FEW, dps, *given)
+    grads = lax.cond(most[0, 0] < FEW + 0.5, lambda: tuple(grads), lambda: tuple(whole(ALL, dps, *given)[:4]))
+    return tuple(g[None] for g in grads)
 
 
 def solution(mesh):

time: 161 us -> 141 us (0.88)
  Pallas kernels: 154 us -> 133 us
    pallas_call x3 -> x1, Pallas kernels: 154 us -> 133 us  [whole(): pl.pallas_call(functools.partial(whole_kernel, slots, dps), in_specs=[sme...]
    unnamed x12 -> x18, local copies, waits for them, and re-layouts: 0.03 us -> 5.19 us
    broadcast_in_dim x2 -> x0, local copies, waits for them, and re-layouts: 2.72 us -> none  [body(): alog, bias = (a_log[:, None], dt_bias[:, None])]
where the time goes in v4:
time: 141 us
  Pallas kernels  133 us (94%)
  local copies, waits for them, and re-layouts  6.38 us (5%)
  between operations  1.42 us (1%)
    pallas_call x1, Pallas kernels, whole(): pl.pallas_call(functools.partial(whole_kernel, slots, dps), in_specs=[sme...  133 us
    unnamed x18, local copies, waits for them, and re-layouts  5.19 us

profile of v4, /device:TPU:16, one launch (start us, length us, event | category | flops | bytes accessed | tf_op | source)
XLA Modules:
  0.0 141.1 jit_solution(5067676466809757360)
XLA Ops:
  0.6 0.0 copy-start
  0.6 0.0 copy-start.1
  0.7 0.0 copy-start.2
  0.7 0.0 copy-start.3
  0.7 0.0 copy-start.4
  0.7 0.0 copy-start.5
  0.7 0.0 copy-start.6
  0.7 133.2 %whole_7.1 = (bf16[256,4096]{1,0:T(8,128)(2,1)}, f32[64,256]{1,0:T(8,128)S(1)}, f32[256,256]{1,0:T(8,128)S(1)}, f32[256,256]{1,0:T(8,128)S(1)}, f32[8,128]{1,0:T(8,128)}) custom-call(s32[32]{0:T(128)} %parent_ref.1, f32[64]{0:T(128)} %alog_ref.1, f32[64]{0:T(128)} %bias_ref.1, f32[64]{0:T(128)} %skip_ref.1, bf16[256,4096]{1,0:T(8,128)(2,1)} %bitcast.10, ...), custom_call_target="tpu_custom_call" | custom-call | tf_op jit(solution)/shard_map/whole_7/pallas_call | solution.py:536
  133.9 1.2 slice.3
  135.7 0.0 copy-done
  135.7 0.0 copy-done.1
  135.7 0.0 copy-done.2
  135.7 0.0 copy-done.3
  135.8 0.0 copy-done.4
  135.8 0.0 copy-done.5
  135.8 0.0 copy-done.6
  135.8 0.2 conditional.1
  136.0 3.1 %copy.25 = bf16[1,256,4096]{2,1,0:T(8,128)(2,1)} copy(bf16[1,256,4096]{2,1,0:T(8,128)(2,1)} %bitcast.14) | data formatting | bytes 4194304
  139.1 0.6 copy.26
  139.7 0.7 copy.27
  140.4 0.7 copy.28
Async XLA Ops:
  0.6 135.1 %copy-start = (bf16[1,256,256]{2,1,0:T(8,128)(2,1)S(1)}, bf16[1,256,256]{2,1,0:T(8,128)(2,1)}, u32[]{:S(2)}) copy-start(bf16[1,256,256]{2,1,0:T(8,128)(2,1)} %param.14) | copy-start | bytes 393220
  0.6 135.1 %copy-start.1 = (bf16[1,256,256]{2,1,0:T(8,128)(2,1)S(1)}, bf16[1,256,256]{2,1,0:T(8,128)(2,1)}, u32[]{:S(2)}) copy-start(bf16[1,256,256]{2,1,0:T(8,128)(2,1)} %param.15) | copy-start | bytes 393220
  0.7 135.1 %copy-start.2 = (f32[1,64,256]{2,1,0:T(8,128)S(1)}, f32[1,64,256]{2,1,0:T(8,128)}, u32[]{:S(2)}) copy-start(f32[1,64,256]{2,1,0:T(8,128)} %param.13) | copy-start | bytes 196612
  0.7 135.1 %copy-start.3 = (s32[32]{0:T(128)S(1)}, s32[32]{0:T(128)}, u32[]{:S(2)}) copy-start(s32[32]{0:T(128)} %parent_ref.1) | copy-start | bytes 388
  0.7 135.1 %copy-start.4 = (f32[64]{0:T(128)S(1)}, f32[64]{0:T(128)}, u32[]{:S(2)}) copy-start(f32[64]{0:T(128)} %alog_ref.1) | copy-start | bytes 772
  0.7 135.1 %copy-start.5 = (f32[64]{0:T(128)S(1)}, f32[64]{0:T(128)}, u32[]{:S(2)}) copy-start(f32[64]{0:T(128)} %bias_ref.1) | copy-start | bytes 772
  0.7 135.1 %copy-start.6 = (f32[64]{0:T(128)S(1)}, f32[64]{0:T(128)}, u32[]{:S(2)}) copy-start(f32[64]{0:T(128)} %skip_ref.1) | copy-start | bytes 772

commit v5 on v4

--- a/solution.py
+++ b/solution.py
@@ -11,8 +11,9 @@
 STATE = 128
 NX = 4
 NZ = 8
-ARM = 4
-LAG = 3
+PIECES = 4
+ARM = 5
+LAG = 4
 F32 = jnp.float32
 BF16 = jnp.bfloat16
 
@@ -181,14 +182,37 @@
         gc_ref[:, group] = (sumc[g] + dot(b_ref[:, group], low, 0, 1)).T
 
 
-def arms(near, pick):
-    def furthest(v):
-        return jnp.max(jnp.where(near, v, 0), axis=1, keepdims=True)
-
-    up = furthest(jnp.where(pick < ARM, pick, 0))
-    down = furthest(jnp.where(pick > ARM, NZ - pick, 0))
-    both = furthest(jnp.where(pick == ARM, 1, 0)) > 0
-    return jnp.where(both & (up >= down), ARM, up), jnp.where(both & (up < down), ARM, down)
+def arms(near, sub, lane):
+    pick = (lane - sub) & (NZ - 1)
+    ups, downs, covers = [], [], []
+    for k in range(NZ - ARM - 1, ARM + 1):
+        up = jnp.max(jnp.where(near & (pick <= k), pick, 0), axis=1, keepdims=True)
+        down = jnp.max(jnp.where(near & (pick > k), NZ - pick, 0), axis=1, keepdims=True)
+        used = (((lane - sub) & (NZ - 1)) < up) | (((sub - 1 - lane) & (NZ - 1)) < down)
+        ups.append(jnp.broadcast_to(up, sub.shape))
+        downs.append(jnp.broadcast_to(down, sub.shape))
+        covers.append(jnp.where(used & (lane < NZ), 1.0, 0.0))
+    up, down, now = ups[0], downs[0], covers[0]
+    least = jnp.sum(now, axis=1, keepdims=True)
+    for k in range(1, len(covers)):
+        steps = jnp.sum(covers[k], axis=1, keepdims=True)
+        less = jnp.broadcast_to(steps < least, sub.shape)
+        up, down, now = jnp.where(less, ups[k], up), jnp.where(less, downs[k], down), jnp.where(less, covers[k], now)
+        least = jnp.minimum(steps, least)
+    for _ in range(3):
+        load = jnp.sum(now, axis=0, keepdims=True) - now
+        costs = []
+        for cover in covers:
+            cost = jnp.where(lane < NZ, jnp.exp((load + cover) * 1.3862944), 0.0)
+            costs.append(jnp.broadcast_to(jnp.sum(cost, axis=1, keepdims=True), sub.shape))
+        best = functools.reduce(jnp.minimum, costs)
+        best = jnp.min(best, axis=0, keepdims=True)
+        names = [jnp.where(cost == best, k * NX * NZ + sub, NX * NZ * NZ) for k, cost in enumerate(costs)]
+        name = jnp.min(functools.reduce(jnp.minimum, names), axis=0, keepdims=True)
+        for k in range(len(covers)):
+            hit = name == k * NX * NZ + sub
+            up, down, now = jnp.where(hit, ups[k], up), jnp.where(hit, downs[k], down), jnp.where(hit, covers[k], now)
+    return up, down
 
 
 def whole_kernel(slots, dps, parent_ref, alog_ref, bias_ref, skip_ref, x_ref, dy_ref, raw_ref, b_ref, c_ref,
@@ -198,8 +222,8 @@
                  in_send, in_recv, z_send, z_recv, out_send, out_recv, out_own, carry_send, carry_recv):
     nodes = NX * NZ
     part = own_ref.shape[0] // NX
-    half = HEAD_DIM // 2
-    chunks = part * 2
+    size = HEAD_DIM // PIECES
+    chunks = part * PIECES
     rounds = chunks + LAG * (ARM - 1)
     pairs = own_ref.shape[0] // 2
     groups = score.shape[0]
@@ -294,9 +318,7 @@
         par_row = jnp.where(lane == n, parent_ref[n], par_row)
     is_root = par_col < 0
     near = (par_row == sub) | (is_root & (lane < nodes))
-    up, down = arms(near, (lane - sub) & (NZ - 1))
-    up = jnp.broadcast_to(up, (nodes, lanes))
-    down = jnp.broadcast_to(down, (nodes, lanes))
+    up, down = arms(near, sub, lane)
 
     def one(v):
         return jnp.where(v, 1.0, 0.0)
@@ -393,24 +415,27 @@
     def own_out(hd):
         return pltpu.make_async_copy(res.at[x, hd], both_ref.at[x * part + hd], out_own.at[hd])
 
+    def part_of(chunk):
+        return pl.ds(pl.multiple_of(lax.rem(chunk, PIECES) * size, size), size)
+
     def piece(k, chunk, kind):
-        rows = pl.ds(pl.multiple_of(lax.rem(chunk, 2) * half, half), half)
-        return xin[k, chunk // 2, kind, rows, :]
+        return xin[k, chunk // PIECES, kind, part_of(chunk), :]
 
     last = LAG * ARM
 
-    late = last + 2 * NX - 2
-
-    @pl.loop(0, pairs + late)
+    steps = PIECES // 2
+    late = last + 2 * PIECES + 3
+
+    @pl.loop(0, steps * (pairs - 1) + late + 1)
     def _(r):
         @pl.when((r >= LAG) & (r < rounds + LAG))
         def _():
             for way in range(2):
                 z_copy(way, r - LAG).wait_recv()
 
-        @pl.when((lax.rem(r, 2) == 0) & (r < chunks))
-        def _():
-            hd = r // 2
+        @pl.when((lax.rem(r, PIECES) == 0) & (r < chunks))
+        def _():
+            hd = r // PIECES
 
             for k in range(1, NX):
                 in_copy(hd, k).wait_recv()
@@ -435,8 +460,7 @@
                     chunk = jnp.clip(r - LAG * (ARM - 1 - d), 0, chunks - 1)
                     for k in range(NX):
                         acc += remote[1 - way, d, k] * piece(k, chunk, 1)[None]
-                    rows = pl.ds(pl.multiple_of(lax.rem(chunk, 2) * half, half), half)
-                    acc += remote[1 - way, d, NX] * extra[chunk // 2, rows, :][None]
+                    acc += remote[1 - way, d, NX] * extra[chunk // PIECES, part_of(chunk), :][None]
                 for j in range(slots):
                     acc += relay[way, j] * got[way, r, j][None]
                 put[way, lax.rem(r, 3)] = acc
@@ -445,8 +469,8 @@
         @pl.when((r >= last) & (r < chunks + last))
         def _():
             c = r - last
-            hd = c // 2
-            rows = pl.ds(pl.multiple_of(lax.rem(c, 2) * half, half), half)
+            hd = c // PIECES
+            rows = part_of(c)
             begin = here[0] * piece(0, c, 0)[None]
             for k in range(1, NX):
                 begin += here[k] * piece(k, c, 0)[None]
@@ -464,29 +488,30 @@
                 res[k, hd, 0, rows, :] = begin[k] + scale[k, x * part + hd] * begin[NX]
                 res[k, hd, 1, rows, :] = end[k]
 
-            @pl.when(lax.rem(c, 2) == 1)
+            @pl.when(lax.rem(c, PIECES) == PIECES - 1)
             def _():
                 for k in range(1, NX):
                     out_copy(hd, k).start()
                 own_out(hd).start()
 
-        @pl.when(r + first < pairs)
-        def _():
-            summary(r + first)
-
-            @pl.when(lax.rem(r + first, NX) == NX - 1)
+        @pl.when((lax.rem(r, steps) == 1) & (r // steps + first < pairs))
+        def _():
+            index = r // steps + first
+            summary(index)
+
+            @pl.when(lax.rem(index, NX) == NX - 1)
             def _():
-                start_in(2 * ((r + first) // NX))
-                start_in(2 * ((r + first) // NX) + 1)
-
-        @pl.when(r < pairs)
-        def _():
-            pair, side, group = place(r)
+                start_in(2 * (index // NX))
+                start_in(2 * (index // NX) + 1)
+
+        @pl.when((lax.rem(r, steps) == 0) & (r // steps < pairs))
+        def _():
+            pair, side, group = place(r // steps)
             inner_pair(pair, group, skip_ref, dy_ref, xt_s, dyt_s, rise_s, fall_s, dx_s, row_s, col_s, score, summed)
 
-        @pl.when(r >= late)
-        def _():
-            index = r - late
+        @pl.when((r >= late) & (lax.rem(r - late, steps) == 0))
+        def _():
+            index = (r - late) // steps
 
             @pl.when(lax.rem(index, NX) == 0)
             def _():
@@ -526,8 +551,8 @@
     pairs = heads // 2
     groups = b.shape[1] // STATE
     part = heads // NX
-    half = HEAD_DIM // 2
-    rounds = part * 2 + LAG * (ARM - 1)
+    size = HEAD_DIM // PIECES
+    rounds = part * PIECES + LAG * (ARM - 1)
     dma = pltpu.SemaphoreType.DMA
     vmem = pl.BlockSpec(memory_space=pltpu.VMEM)
     smem = pl.BlockSpec(memory_space=pltpu.SMEM)
@@ -568,8 +593,8 @@
             dma((dps,)),
             pltpu.VMEM((NX, part, 2, HEAD_DIM, STATE), F32),
             pltpu.VMEM((part, HEAD_DIM, STATE), F32),
-            pltpu.VMEM((2, rounds + LAG, slots, half, STATE), F32),
-            pltpu.VMEM((2, 3, slots, half, STATE), F32),
+            pltpu.VMEM((2, rounds + LAG, slots, size, STATE), F32),
+            pltpu.VMEM((2, 3, slots, size, STATE), F32),
             pltpu.VMEM((NX, part, 2, HEAD_DIM, STATE), F32),
             pltpu.VMEM((1, 1, STATE), F32),
             pltpu.VMEM((NX * NZ, 1, STATE), F32),
@@ -593,7 +618,27 @@
     )(parent, alog, bias, skip, x, dy, raw, b, c)
 
 
-FEW = 7
+def settle_kernel(n, *refs):
+    for i in range(n):
+        refs[n + i][...] = refs[i][...]
+
+
+def settle(arrays):
+    n, parts = len(arrays), 4
+    spots = [pl.BlockSpec((a.shape[0] // parts, a.shape[1]), lambda i: (i, 0)) for a in arrays]
+    return tuple(
+        pl.pallas_call(
+            functools.partial(settle_kernel, n),
+            grid=(parts,),
+            in_specs=spots,
+            out_specs=spots,
+            out_shape=[sds(a.shape, a.dtype) for a in arrays],
+            name="settle",
+        )(*arrays)
+    )
+
+
+FEW = 6
 ALL = 13
 
 
@@ -601,7 +646,7 @@
     given = (parent, a_log, dt_bias, skip, inputs[0], grad_out[0], dt_raw[0], b_proj[0], c_proj[0])
     dps = lax.axis_size("dp")
     *grads, most = whole(FEW, dps, *given)
-    grads = lax.cond(most[0, 0] < FEW + 0.5, lambda: tuple(grads), lambda: tuple(whole(ALL, dps, *given)[:4]))
+    grads = lax.cond(most[0, 0] < FEW + 0.5, lambda: settle(grads), lambda: settle(whole(ALL, dps, *given)[:4]))
     return tuple(g[None] for g in grads)
 
 

time: 141 us -> 141 us (level)
  local copies, waits for them, and re-layouts: 6.38 us -> 1.22 us
  Pallas kernels: 133 us -> 138 us
    unnamed x18 -> x14, local copies, waits for them, and re-layouts: 5.19 us -> 0.03 us
    pallas_call x0 -> x1, Pallas kernels: none -> 3.89 us  [settle(): pl.pallas_call(functools.partial(settle_kernel, n), grid=(parts,), in_spe...]
where the time goes in v5:
time: 141 us; the launch traced here: 140 us
  Pallas kernels  138 us (98%)
  between operations  1.41 us (1%)
    pallas_call x1, Pallas kernels, whole(): pl.pallas_call(functools.partial(whole_kernel, slots, dps), in_specs=[sme...  134 us
    pallas_call x1, Pallas kernels, settle(): pl.pallas_call(functools.partial(settle_kernel, n), grid=(parts,), in_spe...  3.89 us

profile of v5, /device:TPU:16, one launch (start us, length us, event | category | flops | bytes accessed | tf_op | source)
XLA Modules:
  0.0 140.4 jit_solution(11930964036935639385)
XLA Ops:
  0.6 0.0 copy-start
  0.6 0.0 copy-start.1
  0.7 0.0 copy-start.2
  0.7 0.0 copy-start.3
  0.7 0.0 copy-start.4
  0.7 0.0 copy-start.5
  0.7 0.0 copy-start.6
  0.7 133.7 %whole_6.1 = (bf16[256,4096]{1,0:T(8,128)(2,1)}, f32[64,256]{1,0:T(8,128)S(1)}, f32[256,256]{1,0:T(8,128)S(1)}, f32[256,256]{1,0:T(8,128)S(1)}, f32[8,128]{1,0:T(8,128)}) custom-call(s32[32]{0:T(128)} %parent_ref.1, f32[64]{0:T(128)} %alog_ref.1, f32[64]{0:T(128)} %bias_ref.1, f32[64]{0:T(128)} %skip_ref.1, bf16[256,4096]{1,0:T(8,128)(2,1)} %bitcast.10, ...), custom_call_target="tpu_custom_call" | custom-call | tf_op jit(solution)/shard_map/whole_6/pallas_call | solution.py:561
  134.4 1.2 slice.3
  136.3 0.0 copy-done
  136.3 0.0 copy-done.1
  136.3 0.0 copy-done.2
  136.3 0.0 copy-done.3
  136.3 0.0 copy-done.4
  136.3 0.0 copy-done.5
  136.3 0.0 copy-done.6
  136.3 4.1 %conditional.1 = ((bf16[256,4096]{1,0:T(8,128)(2,1)}, f32[64,256]{1,0:T(8,128)}, f32[256,256]{1,0:T(8,128)}, f32[256,256]{1,0:T(8,128)})) conditional(s32[]{:T(128)} %bitcast.5, (s32[32]{0:T(128)S(1)}, f32[64]{0:T(128)S(1)}, f32[64]{0:T(128)S(1)}, f32[64]{0:T(128)S(1)}, bf16[256,4096]{1,0:T(8,128)(2,1)}, ...), branch_computations={%region_0.0_spmd.clone, %region_1.0_spmd.clone} | conditional | bytes 8 | solution.py:649
  136.5 3.9 %settle.3 = (bf16[256,4096]{1,0:T(8,128)(2,1)}, f32[64,256]{1,0:T(8,128)}, f32[256,256]{1,0:T(8,128)}, f32[256,256]{1,0:T(8,128)}) custom-call(bf16[256,4096]{1,0:T(8,128)(2,1)} %get-tuple-element.97.refs_0_, f32[64,256]{1,0:T(8,128)S(1)} %get-tuple-element.98.refs_1_, f32[256,256]{1,0:T(8,128)S(1)} %get-tuple-element.99.refs_2_, ...), custom_call_target="tpu_custom_call" | custom-call | tf_op jit(solution)/shard_map/cond/branch_1_fun/settle/pallas_call | solution.py:630
Async XLA Ops:
  0.6 135.6 %copy-start = (bf16[1,256,256]{2,1,0:T(8,128)(2,1)S(1)}, bf16[1,256,256]{2,1,0:T(8,128)(2,1)}, u32[]{:S(2)}) copy-start(bf16[1,256,256]{2,1,0:T(8,128)(2,1)} %param.14) | copy-start | bytes 393220
  0.6 135.6 %copy-start.1 = (bf16[1,256,256]{2,1,0:T(8,128)(2,1)S(1)}, bf16[1,256,256]{2,1,0:T(8,128)(2,1)}, u32[]{:S(2)}) copy-start(bf16[1,256,256]{2,1,0:T(8,128)(2,1)} %param.15) | copy-start | bytes 393220
  0.7 135.6 %copy-start.2 = (f32[1,64,256]{2,1,0:T(8,128)S(1)}, f32[1,64,256]{2,1,0:T(8,128)}, u32[]{:S(2)}) copy-start(f32[1,64,256]{2,1,0:T(8,128)} %param.13) | copy-start | bytes 196612
  0.7 135.6 %copy-start.3 = (s32[32]{0:T(128)S(1)}, s32[32]{0:T(128)}, u32[]{:S(2)}) copy-start(s32[32]{0:T(128)} %parent_ref.1) | copy-start | bytes 388
  0.7 135.6 %copy-start.4 = (f32[64]{0:T(128)S(1)}, f32[64]{0:T(128)}, u32[]{:S(2)}) copy-start(f32[64]{0:T(128)} %alog_ref.1) | copy-start | bytes 772
  0.7 135.6 %copy-start.5 = (f32[64]{0:T(128)S(1)}, f32[64]{0:T(128)}, u32[]{:S(2)}) copy-start(f32[64]{0:T(128)} %bias_ref.1) | copy-start | bytes 772
  0.7 135.6 %copy-start.6 = (f32[64]{0:T(128)S(1)}, f32[64]{0:T(128)}, u32[]{:S(2)}) copy-start(f32[64]{0:T(128)} %skip_ref.1) | copy-start | bytes 772

commit v6 on v5

--- a/solution.py
+++ b/solution.py
@@ -11,9 +11,9 @@
 STATE = 128
 NX = 4
 NZ = 8
-PIECES = 4
+PIECES = 2
 ARM = 5
-LAG = 4
+LAG = 3
 F32 = jnp.float32
 BF16 = jnp.bfloat16
 
@@ -423,10 +423,9 @@
 
     last = LAG * ARM
 
-    steps = PIECES // 2
-    late = last + 2 * PIECES + 3
-
-    @pl.loop(0, steps * (pairs - 1) + late + 1)
+    late = last + 2 * NX - 2
+
+    @pl.loop(0, pairs + late)
     def _(r):
         @pl.when((r >= LAG) & (r < rounds + LAG))
         def _():
@@ -494,24 +493,23 @@
                     out_copy(hd, k).start()
                 own_out(hd).start()
 
-        @pl.when((lax.rem(r, steps) == 1) & (r // steps + first < pairs))
-        def _():
-            index = r // steps + first
-            summary(index)
-
-            @pl.when(lax.rem(index, NX) == NX - 1)
+        @pl.when(r + first < pairs)
+        def _():
+            summary(r + first)
+
+            @pl.when(lax.rem(r + first, NX) == NX - 1)
             def _():
-                start_in(2 * (index // NX))
-                start_in(2 * (index // NX) + 1)
-
-        @pl.when((lax.rem(r, steps) == 0) & (r // steps < pairs))
-        def _():
-            pair, side, group = place(r // steps)
+                start_in(2 * ((r + first) // NX))
+                start_in(2 * ((r + first) // NX) + 1)
+
+        @pl.when(r < pairs)
+        def _():
+            pair, side, group = place(r)
             inner_pair(pair, group, skip_ref, dy_ref, xt_s, dyt_s, rise_s, fall_s, dx_s, row_s, col_s, score, summed)
 
-        @pl.when((r >= late) & (lax.rem(r - late, steps) == 0))
-        def _():
-            index = (r - late) // steps
+        @pl.when(r >= late)
+        def _():
+            index = r - late
 
             @pl.when(lax.rem(index, NX) == 0)
             def _():

time: 141 us -> 137 us (0.972)
  Pallas kernels: 138 us -> 134 us
    pallas_call x1, Pallas kernels: 134 us -> 130 us  [whole(): pl.pallas_call(functools.partial(whole_kernel, slots, dps), in_specs=[sme...]
where the time goes in v6:
time: 137 us
  Pallas kernels  134 us (98%)
  between operations  1.41 us (1%)
    pallas_call x1, Pallas kernels, whole(): pl.pallas_call(functools.partial(whole_kernel, slots, dps), in_specs=[sme...  130 us
    pallas_call x1, Pallas kernels, settle(): pl.pallas_call(functools.partial(settle_kernel, n), grid=(parts,), in_spe...  3.89 us

profile of v6, /device:TPU:16, one launch (start us, length us, event | category | flops | bytes accessed | tf_op | source)
XLA Modules:
  0.0 136.7 jit_solution(13544700960665470655)
XLA Ops:
  0.6 0.0 copy-start
  0.6 0.0 copy-start.1
  0.7 0.0 copy-start.2
  0.7 0.0 copy-start.3
  0.7 0.0 copy-start.4
  0.7 0.0 copy-start.5
  0.7 0.0 copy-start.6
  0.7 130.0 %whole_6.1 = (bf16[256,4096]{1,0:T(8,128)(2,1)}, f32[64,256]{1,0:T(8,128)S(1)}, f32[256,256]{1,0:T(8,128)S(1)}, f32[256,256]{1,0:T(8,128)S(1)}, f32[8,128]{1,0:T(8,128)}) custom-call(s32[32]{0:T(128)} %parent_ref.1, f32[64]{0:T(128)} %alog_ref.1, f32[64]{0:T(128)} %bias_ref.1, f32[64]{0:T(128)} %skip_ref.1, bf16[256,4096]{1,0:T(8,128)(2,1)} %bitcast.10, ...), custom_call_target="tpu_custom_call" | custom-call | tf_op jit(solution)/shard_map/whole_6/pallas_call | solution.py:559
  130.7 1.2 slice.3
  132.6 0.0 copy-done
  132.6 0.0 copy-done.1
  132.6 0.0 copy-done.2
  132.6 0.0 copy-done.3
  132.6 0.0 copy-done.4
  132.6 0.0 copy-done.5
  132.6 0.0 copy-done.6
  132.7 4.1 %conditional.1 = ((bf16[256,4096]{1,0:T(8,128)(2,1)}, f32[64,256]{1,0:T(8,128)}, f32[256,256]{1,0:T(8,128)}, f32[256,256]{1,0:T(8,128)})) conditional(s32[]{:T(128)} %bitcast.5, (s32[32]{0:T(128)S(1)}, f32[64]{0:T(128)S(1)}, f32[64]{0:T(128)S(1)}, f32[64]{0:T(128)S(1)}, bf16[256,4096]{1,0:T(8,128)(2,1)}, ...), branch_computations={%region_0.0_spmd.clone, %region_1.0_spmd.clone} | conditional | bytes 8 | solution.py:647
  132.9 3.9 %settle.3 = (bf16[256,4096]{1,0:T(8,128)(2,1)}, f32[64,256]{1,0:T(8,128)}, f32[256,256]{1,0:T(8,128)}, f32[256,256]{1,0:T(8,128)}) custom-call(bf16[256,4096]{1,0:T(8,128)(2,1)} %get-tuple-element.97.refs_0_, f32[64,256]{1,0:T(8,128)S(1)} %get-tuple-element.98.refs_1_, f32[256,256]{1,0:T(8,128)S(1)} %get-tuple-element.99.refs_2_, ...), custom_call_target="tpu_custom_call" | custom-call | tf_op jit(solution)/shard_map/cond/branch_1_fun/settle/pallas_call | solution.py:628
Async XLA Ops:
  0.6 132.0 %copy-start = (bf16[1,256,256]{2,1,0:T(8,128)(2,1)S(1)}, bf16[1,256,256]{2,1,0:T(8,128)(2,1)}, u32[]{:S(2)}) copy-start(bf16[1,256,256]{2,1,0:T(8,128)(2,1)} %param.14) | copy-start | bytes 393220
  0.6 132.0 %copy-start.1 = (bf16[1,256,256]{2,1,0:T(8,128)(2,1)S(1)}, bf16[1,256,256]{2,1,0:T(8,128)(2,1)}, u32[]{:S(2)}) copy-start(bf16[1,256,256]{2,1,0:T(8,128)(2,1)} %param.15) | copy-start | bytes 393220
  0.7 132.0 %copy-start.2 = (f32[1,64,256]{2,1,0:T(8,128)S(1)}, f32[1,64,256]{2,1,0:T(8,128)}, u32[]{:S(2)}) copy-start(f32[1,64,256]{2,1,0:T(8,128)} %param.13) | copy-start | bytes 196612
  0.7 132.0 %copy-start.3 = (s32[32]{0:T(128)S(1)}, s32[32]{0:T(128)}, u32[]{:S(2)}) copy-start(s32[32]{0:T(128)} %parent_ref.1) | copy-start | bytes 388
  0.7 132.0 %copy-start.4 = (f32[64]{0:T(128)S(1)}, f32[64]{0:T(128)}, u32[]{:S(2)}) copy-start(f32[64]{0:T(128)} %alog_ref.1) | copy-start | bytes 772
  0.7 132.0 %copy-start.5 = (f32[64]{0:T(128)S(1)}, f32[64]{0:T(128)}, u32[]{:S(2)}) copy-start(f32[64]{0:T(128)} %bias_ref.1) | copy-start | bytes 772
  0.7 132.0 %copy-start.6 = (f32[64]{0:T(128)S(1)}, f32[64]{0:T(128)}, u32[]{:S(2)}) copy-start(f32[64]{0:T(128)} %skip_ref.1) | copy-start | bytes 772
